TPU v7x, 768 devices: a whole 4x8x12 slice. The times are simulated.
768 devices in a mesh: prow: 96 (over z, x, core), pcol: 8 (over y).
Axes of the slice: x: 4, y: 8, z: 12, core: 2. Of those that a mesh axis runs over, the one named last changes fastest.
Arguments:
- dof_values: float32 [9, 56, 98304], P(None, None, ('prow', 'pcol')), may hold values from -6 to 6
- grad_matrix: float32 [3, 56, 56], replicated, may hold values from -0.75 to 0.75
- stiff_matrix: float32 [3, 56, 56], replicated, may hold values from -0.1875 to 0.1875
- face_proj: float32 [4, 21, 56], replicated, may hold values from -0.75 to 0.75
- face_lift: float32 [4, 56, 21], replicated, may hold values from -0.3125 to 0.3125
- rotate: float32 [3, 21, 21], replicated, may hold values from -1.25 to 1.25
- material: float32 [16, 3], replicated, may hold values from 0.5 to 2
- material_id: int32 [98304], P(('prow', 'pcol')), may hold values from 0 to 15
- inv_jacobian: float32 [3, 3, 98304], P(None, None, ('prow', 'pcol')), may hold values from -3 to 3
- normals: float32 [4, 3, 98304], P(None, None, ('prow', 'pcol')), may hold values from -2 to 2
- orientation: int32 [4, 98304], P(None, ('prow', 'pcol')), may hold values from 0 to 2
- neighbour: int32 [4, 98304], P(None, ('prow', 'pcol')), may hold values from -1 to 127, as said below
- neighbour_face: int32 [4, 98304], P(None, ('prow', 'pcol')), may hold values from 0 to 3, as said below
- send_list: int32 [96, 8, 8, 24], P('prow', 'pcol'), may hold values from -1 to 511, as said below
- recv_list: int32 [96, 8, 8, 24], P('prow', 'pcol'), may hold values from -1 to 511, as said below
Outputs:
- new_dofs: float32 [9, 56, 98304], P(None, None, ('prow', 'pcol'))
Inputs may be any that keep to these rules, and one draw needn't show every extreme that they name: `neighbour`: -1 where the face has no neighbour in the same partition; otherwise faces are matched in pairs: the element neighbour[f, e] lists e back across its face neighbour_face[f, e]. `neighbour_face`: 0 where neighbour is -1. `send_list`: entry (r, c, d, m) is a local face id of partition (r, c) whose neighbour lies in the partition at offset d, or -1; live slots of a direction come first, each such face appears once, and the live count of (r, c, d) equals that of the partner's direction 7 - d; directions leaving the grid have none. Some partition has 24 live slots in all eight directions, and every live count is at most 24. `recv_list`: entry (r, c, d, m) is the local face id of partition (r, c) that meets the face in slot m of the send_list of the partner at offset d for direction 7 - d, or -1 where that slot is empty; its live slots hold the same faces as send_list of (r, c, d) in another order.
All inputs are finite; a program needn't handle non-finite values.
Results may differ from a plain program's by a relative error of at most 0.0003.
Values sent between devices are 32-bit elements; how exact they have to be, the bound alone decides.
A program may use at most 32 MiB of HBM per device.

v0:
```python
import jax
import jax.numpy as jnp
from jax import lax
from jax.sharding import PartitionSpec as P

ORDER = 6
STEPS = 2


exact_mode = lax.Precision.HIGHEST
time_step = 0.8
OFFSETS = ((-1, -1), (-1, 0), (-1, 1), (0, -1), (0, 1), (1, -1), (1, 0), (1, 1))
ENTRIES = (
    (0, 0, 6, 0),
    (0, 1, 6, 1),
    (0, 2, 6, 1),
    (0, 3, 7, 2),
    (0, 5, 8, 2),
    (0, 6, 0, 3),
    (0, 7, 3, 3),
    (0, 8, 5, 3),
    (1, 0, 7, 1),
    (1, 1, 7, 0),
    (1, 2, 7, 1),
    (1, 3, 6, 2),
    (1, 4, 8, 2),
    (1, 6, 3, 3),
    (1, 7, 1, 3),
    (1, 8, 4, 3),
    (2, 0, 8, 1),
    (2, 1, 8, 1),
    (2, 2, 8, 0),
    (2, 4, 7, 2),
    (2, 5, 6, 2),
    (2, 6, 5, 3),
    (2, 7, 4, 3),
    (2, 8, 2, 3),
)


def shifted(x, axis, by):
    devices = lax.axis_size(axis)
    pairs = [(i, i + by) for i in range(devices) if 0 <= i + by < devices]
    return lax.ppermute(x, axis, pairs)


def element_params(material, material_id, normals):
    id_range = jnp.arange(material.shape[0], dtype=jnp.int32)
    onehot = (material_id[None, :] == id_range[:, None]).astype(material.dtype)
    params = jnp.dot(material.T, onehot, precision=exact_mode)
    density, lame_first, shear_modulus = (params[0], params[1], params[2])
    values = (-(lame_first + 2.0 * shear_modulus), -lame_first, -shear_modulus, -1.0 / density)
    wave_speed = jnp.sqrt((lame_first + 2.0 * shear_modulus) / density) * jnp.sum(
        jnp.abs(normals), axis=1
    )
    return (values, wave_speed)


def elastic_apply(parts, values):
    result = [None] * 9
    for comp_axis, row_index, col_index, kind_index in ENTRIES:
        term = values[kind_index] * parts[comp_axis][col_index]
        result[row_index] = term if result[row_index] is None else result[row_index] + term
    return jnp.stack(result, axis=0)


def star_apply(slopes, inv_jacobian, values):
    parts = [jnp.sum(inv_jacobian[:, k][:, None, None, :] * slopes, axis=0) for k in range(3)]
    return elastic_apply(parts, values)


def predict(current, inv_jacobian, values, grad_matrix):
    derivative = current
    integrated = time_step * current
    factor = time_step
    for power_level in range(1, ORDER):
        slopes = jnp.einsum("dab,qbe->dqae", grad_matrix, derivative, precision=exact_mode)
        derivative = -star_apply(slopes, inv_jacobian, values)
        factor = factor * time_step / (power_level + 1)
        integrated = integrated + factor * derivative
    return integrated


def local_part(current, inv_jacobian, values, grad_matrix, stiff_matrix, face_proj):
    integrated = predict(current, inv_jacobian, values, grad_matrix)
    slopes = jnp.einsum("dab,qbe->dqae", stiff_matrix, integrated, precision=exact_mode)
    volume = star_apply(slopes, inv_jacobian, values)
    face_data = jnp.einsum("fib,qbe->qife", face_proj, integrated, precision=exact_mode)
    return (volume, face_data)


def face_update(
    current,
    volume,
    face_data,
    neighbour_data,
    orientation,
    normals,
    values,
    wave_speed,
    rotate,
    face_lift,
):
    turned = jnp.einsum("hil,qlfe->hqife", rotate, neighbour_data, precision=exact_mode)
    chosen = (orientation[None] == jnp.arange(3, dtype=jnp.int32)[:, None, None]).astype(
        current.dtype
    )
    turned = jnp.sum(turned * chosen[:, None, None, :, :], axis=0)
    both = face_data + turned
    apart = face_data - turned
    parts = [normals[:, k, :][None, None] * both for k in range(3)]
    flux_total = 0.5 * (elastic_apply(parts, values) + wave_speed[None, None] * apart)
    lifted = jnp.einsum("fai,pife->pae", face_lift, flux_total, precision=exact_mode)
    return current + volume - lifted


def deliver(outgoing):
    forwarded = {}
    for col_step in (-1, 1):
        bundle = jnp.stack(
            [outgoing[:, :, OFFSETS.index((row_step, col_step))] for row_step in (-1, 0, 1)], axis=2
        )
        forwarded[col_step] = shifted(bundle, "pcol", col_step)
    pieces = {}
    for col_step in (-1, 1):
        pieces[OFFSETS.index((0, -col_step))] = forwarded[col_step][:, :, 1]
    for row_step in (-1, 1):
        bundle = jnp.stack(
            [
                outgoing[:, :, OFFSETS.index((row_step, 0))],
                forwarded[1][:, :, row_step + 1],
                forwarded[-1][:, :, row_step + 1],
            ],
            axis=2,
        )
        arrived_rows = shifted(bundle, "prow", row_step)
        pieces[OFFSETS.index((-row_step, 0))] = arrived_rows[:, :, 0]
        pieces[OFFSETS.index((-row_step, -1))] = arrived_rows[:, :, 1]
        pieces[OFFSETS.index((-row_step, 1))] = arrived_rows[:, :, 2]
    return jnp.stack([pieces[direction] for direction in range(8)], axis=2)


def per_device(
    dof_values,
    grad_matrix,
    stiff_matrix,
    face_proj,
    face_lift,
    rotate,
    material,
    material_id,
    inv_jacobian,
    normals,
    orientation,
    neighbour,
    neighbour_face,
    send_list,
    recv_list,
):
    elem_count = dof_values.shape[2]
    face_width = face_proj.shape[1]
    values, wave_speed = element_params(material, material_id, normals)
    inside = (neighbour >= 0).reshape(-1)
    local_index = (neighbour_face * elem_count + jnp.maximum(neighbour, 0)).reshape(-1)
    source_ids = send_list[0, 0]
    slot_total = source_ids.shape[1]
    source_index = jnp.maximum(source_ids, 0).reshape(-1)
    source_mask = (source_ids >= 0).reshape(-1).astype(dof_values.dtype)
    targets = jnp.where(recv_list[0, 0] >= 0, recv_list[0, 0], 4 * elem_count).reshape(-1)
    current = dof_values
    for time_index in range(STEPS):
        volume, face_data = local_part(
            current, inv_jacobian, values, grad_matrix, stiff_matrix, face_proj
        )
        flat_faces = face_data.reshape(9, face_width, 4 * elem_count)
        outgoing = (jnp.take(flat_faces, source_index, axis=2) * source_mask).reshape(
            9, face_width, 8, slot_total
        )
        received = deliver(outgoing).reshape(9, face_width, 8 * slot_total)
        arrived = jnp.zeros_like(flat_faces).at[:, :, targets].set(received, mode="drop")
        local_data = jnp.take(flat_faces, local_index, axis=2)
        neighbour_data = jnp.where(inside, local_data, arrived).reshape(
            9, face_width, 4, elem_count
        )
        current = face_update(
            current,
            volume,
            face_data,
            neighbour_data,
            orientation,
            normals,
            values,
            wave_speed,
            rotate,
            face_lift,
        )
    return current


def solution(mesh):
    return jax.shard_map(
        per_device,
        mesh=mesh,
        in_specs=(
            P(None, None, ("prow", "pcol")),
            P(),
            P(),
            P(),
            P(),
            P(),
            P(),
            P(("prow", "pcol")),
            P(None, None, ("prow", "pcol")),
            P(None, None, ("prow", "pcol")),
            P(None, ("prow", "pcol")),
            P(None, ("prow", "pcol")),
            P(None, ("prow", "pcol")),
            P("prow", "pcol", None, None),
            P("prow", "pcol", None, None),
        ),
        out_specs=P(None, None, ("prow", "pcol")),
        check_vma=False,
    )
```

profile of v0, /device:TPU:223, one launch (start us, length us, event | category | flops | bytes accessed | tf_op | source)
XLA Modules:
  0.0 178.3 jit_solution(3503381264493150533)
XLA Ops:
  10.7 2.9 %copy.103 = f32[9,21,4,128]{1,0,3,2:T(8,128)} copy(f32[9,21,4,128]{3,1,2,0:T(8,128)S(1)} %convolution_bitcast_fusion.13) | data formatting | bytes 774144 | tf_op jit(solution)/shard_map/reshape | solution.py:175
  15.3 2.9 %gather_fusion.1 = f32[192,9,21]{2,1,0:T(8,128)S(1)} fusion(f32[9,21,512]{1,0,2:T(8,128)} %bitcast.279, s32[1024]{0:T(1024)S(1)} %get-tuple-element.104), kind=kCustom, calls=%fused_computation.1.clone | custom fusion | bytes 291072 | tf_op jit(solution)/shard_map/jit(_take)/gather | solution.py:176
  20.1 4.4 %collective-permute-start = (f32[9,21,3,24]{3,1,2,0:T(8,128)S(1)}, f32[9,21,3,24]{3,1,2,0:T(8,128)S(1)}, u32[]{:S(2)}, u32[]{:S(2)}) collective-permute-start(f32[9,21,3,24]{3,1,2,0:T(8,128)S(1)} %pad_maximum_fusion), channel_id=1, source_target_pairs={{0,1},{1,2},{2,3},{3,4},{4,5},{5,6},{6,7},{8,9},{9,10},{10,11},{11... | collective-permute-start | bytes 163304 | tf_op jit(solution)/shard_map/ppermute | solution.py:44
  31.0 5.1 %gather_fusion = f32[512,9,21]{2,1,0:T(8,128)} fusion(f32[9,21,512]{1,0,2:T(8,128)} %bitcast.280, s32[1024]{0:T(1024)S(1)} %copy-done.19), kind=kCustom, calls=%fused_computation.clone | custom fusion | bytes 776192 | tf_op jit(solution)/shard_map/jit(_take)/gather | solution.py:181
  38.6 6.9 %collective-permute-start.2 = (f32[9,21,3,24]{3,1,2,0:T(8,128)S(1)}, f32[9,21,3,24]{3,1,2,0:T(8,128)S(1)}, u32[]{:S(2)}, u32[]{:S(2)}) collective-permute-start(f32[9,21,3,24]{3,1,2,0:T(8,128)S(1)} %pad_maximum_fusion.2), channel_id=1, source_target_pairs={{0,8},{8,16},{16,24},{24,32},{32,40},{40,48},{48,56},{56,64},{64,7... | collective-permute-start | bytes 163304 | tf_op jit(solution)/shard_map/ppermute | solution.py:44
  45.7 2.1 %collective-permute-start.3 = (f32[9,21,3,24]{3,1,2,0:T(8,128)S(1)}, f32[9,21,3,24]{3,1,2,0:T(8,128)S(1)}, u32[]{:S(2)}, u32[]{:S(2)}) collective-permute-start(f32[9,21,3,24]{3,1,2,0:T(8,128)S(1)} %pad_maximum_fusion.3), channel_id=1, source_target_pairs={{8,0},{16,8},{24,16},{32,24},{40,32},{48,40},{56,48},{64,56},{72,6... | collective-permute-start | bytes 163304 | tf_op jit(solution)/shard_map/ppermute | solution.py:44
  49.9 7.6 %collective-permute-done.3 = f32[9,21,3,24]{3,1,2,0:T(8,128)S(1)} collective-permute-done((f32[9,21,3,24]{3,1,2,0:T(8,128)S(1)}, f32[9,21,3,24]{3,1,2,0:T(8,128)S(1)}, u32[]{:S(2)}, u32[]{:S(2)}) %collective-permute-start.3) | collective-permute-done | bytes 54464 | tf_op jit(solution)/shard_map/ppermute | solution.py:44
  59.9 2.2 %broadcast.1324.clone = f32[9,21,512]{1,0,2:T(8,128)} broadcast(f32[]{:T(128)} %constant.31.clone.1), dimensions={} | broadcast | bytes 387076 | tf_op jit(solution)/shard_map/broadcast.16
  62.1 21.0 %scatter_fusion = f32[9,21,512]{1,0,2:T(8,128)} fusion(f32[9,21,512]{1,0,2:T(8,128)} %broadcast.1324.clone, s32[192]{0:T(256)} %bitcast.297, f32[192,9,21]{2,1,0:T(8,128)S(1)} %bitcast.284), kind=kCustom, calls=%fused_computation.4 | custom fusion | bytes 436224 | tf_op jit(solution)/shard_map/scatter | solution.py:180
  83.1 5.7 %bitcast_select_fusion.1 = f32[9,21,512]{1,0,2:T(8,128)S(1)} fusion(f32[9,21,512]{1,0,2:T(8,128)} %scatter_fusion, f32[512,9,21]{2,1,0:T(8,128)} %gather_fusion, pred[512]{0:T(512)(128)(4,1)} %get-tuple-element.43, pred[512]{0:T(512)(128)(4,1)} %compare_bitcast_fusion), kind=kLoop, calls=%fused_computation.7 | loop fusion | flops 193536 | bytes 1162240 | tf_op jit(solution)/shard_map/jit(_where)/select_n | solution.py:182
  88.9 3.4 %fusion.19 = f32[9,21,4,128]{3,1,2,0:T(8,128)S(1)} fusion(f32[9,21,4,128,1]{1,0,3,2,4:T(8,128)S(1)} %bitcast.276, f32[3,4,128]{2,0,1:T(4,128)S(1)} %fusion.164, f32[3,21,21]{2,1,0:T(8,128)S(1)} %copy-done.6), kind=kOutput, calls=%fused_computation.19 | convolution fusion | flops 73640448 | bytes 785580 | tf_op jit(solution)/shard_map/hil,qlfe->hqife/dot_general | solution.py:104
  100.1 2.9 %copy.105 = f32[9,21,4,128]{1,0,3,2:T(8,128)} copy(f32[9,21,4,128]{3,1,2,0:T(8,128)S(1)} %convolution_bitcast_fusion.12) | data formatting | bytes 774144 | tf_op jit(solution)/shard_map/reshape | solution.py:175
  103.0 3.0 %gather_fusion.3 = f32[192,9,21]{2,1,0:T(8,128)S(1)} fusion(f32[9,21,512]{1,0,2:T(8,128)} %bitcast.281, s32[1024]{0:T(1024)} %copy-done.24), kind=kCustom, calls=%fused_computation.3.clone | custom fusion | bytes 291072 | tf_op jit(solution)/shard_map/jit(_take)/gather | solution.py:176
  108.3 3.0 %collective-permute-start.4 = (f32[9,21,3,24]{3,1,2,0:T(8,128)S(1)}, f32[9,21,3,24]{3,1,2,0:T(8,128)S(1)}, u32[]{:S(2)}, u32[]{:S(2)}) collective-permute-start(f32[9,21,3,24]{3,1,2,0:T(8,128)S(1)} %pad_maximum_fusion.4), channel_id=1, source_target_pairs={{0,1},{1,2},{2,3},{3,4},{4,5},{5,6},{6,7},{8,9},{9,10},{10,11},{11... | collective-permute-start | bytes 163304 | tf_op jit(solution)/shard_map/ppermute | solution.py:44
  111.4 5.1 %gather_fusion.2 = f32[512,9,21]{2,1,0:T(8,128)} fusion(f32[9,21,512]{1,0,2:T(8,128)} %bitcast.282, s32[1024]{0:T(1024)S(1)} %copy-done.20), kind=kCustom, calls=%fused_computation.2.clone | custom fusion | bytes 776192 | tf_op jit(solution)/shard_map/jit(_take)/gather | solution.py:181
  116.7 2.5 %collective-permute-start.5 = (f32[9,21,3,24]{3,1,2,0:T(8,128)S(1)}, f32[9,21,3,24]{3,1,2,0:T(8,128)S(1)}, u32[]{:S(2)}, u32[]{:S(2)}) collective-permute-start(f32[9,21,3,24]{3,1,2,0:T(8,128)S(1)} %pad_maximum_fusion.5), channel_id=1, source_target_pairs={{1,0},{2,1},{3,2},{4,3},{5,4},{6,5},{7,6},{9,8},{10,9},{11,10},{12... | collective-permute-start | bytes 163304 | tf_op jit(solution)/shard_map/ppermute | solution.py:44
  119.3 6.5 %collective-permute-done.5 = f32[9,21,3,24]{3,1,2,0:T(8,128)S(1)} collective-permute-done((f32[9,21,3,24]{3,1,2,0:T(8,128)S(1)}, f32[9,21,3,24]{3,1,2,0:T(8,128)S(1)}, u32[]{:S(2)}, u32[]{:S(2)}) %collective-permute-start.5) | collective-permute-done | bytes 54464 | tf_op jit(solution)/shard_map/ppermute | solution.py:44
  125.9 4.0 %collective-permute-start.6 = (f32[9,21,3,24]{3,1,2,0:T(8,128)S(1)}, f32[9,21,3,24]{3,1,2,0:T(8,128)S(1)}, u32[]{:S(2)}, u32[]{:S(2)}) collective-permute-start(f32[9,21,3,24]{3,1,2,0:T(8,128)S(1)} %pad_maximum_fusion.6), channel_id=1, source_target_pairs={{0,8},{8,16},{16,24},{24,32},{32,40},{40,48},{48,56},{56,64},{64,7... | collective-permute-start | bytes 163304 | tf_op jit(solution)/shard_map/ppermute | solution.py:44
  130.1 1.9 %collective-permute-start.7 = (f32[9,21,3,24]{3,1,2,0:T(8,128)S(1)}, f32[9,21,3,24]{3,1,2,0:T(8,128)S(1)}, u32[]{:S(2)}, u32[]{:S(2)}) collective-permute-start(f32[9,21,3,24]{3,1,2,0:T(8,128)S(1)} %pad_maximum_fusion.7), channel_id=1, source_target_pairs={{8,0},{16,8},{24,16},{32,24},{40,32},{48,40},{56,48},{64,56},{72,6... | collective-permute-start | bytes 163304 | tf_op jit(solution)/shard_map/ppermute | solution.py:44
  134.2 7.6 %collective-permute-done.7 = f32[9,21,3,24]{3,1,2,0:T(8,128)S(1)} collective-permute-done((f32[9,21,3,24]{3,1,2,0:T(8,128)S(1)}, f32[9,21,3,24]{3,1,2,0:T(8,128)S(1)}, u32[]{:S(2)}, u32[]{:S(2)}) %collective-permute-start.7) | collective-permute-done | bytes 54464 | tf_op jit(solution)/shard_map/ppermute | solution.py:44
  144.3 2.2 %broadcast.1324 = f32[9,21,512]{1,0,2:T(8,128)} broadcast(f32[]{:T(128)} %constant.31.clone.1), dimensions={} | broadcast | bytes 387076 | tf_op jit(solution)/shard_map/broadcast.16
  146.5 20.8 %scatter_fusion.1 = f32[9,21,512]{1,0,2:T(8,128)} fusion(f32[9,21,512]{1,0,2:T(8,128)} %broadcast.1324, s32[192]{0:T(256)S(1)} %bitcast.298, f32[192,9,21]{2,1,0:T(8,128)S(1)} %bitcast.283), kind=kCustom, calls=%fused_computation.5 | custom fusion | bytes 436224 | tf_op jit(solution)/shard_map/scatter | solution.py:180
  167.4 5.8 %bitcast_select_fusion = f32[9,21,512]{1,0,2:T(8,128)S(1)} fusion(f32[9,21,512]{1,0,2:T(8,128)} %scatter_fusion.1, f32[512,9,21]{2,1,0:T(8,128)} %gather_fusion.2, pred[512]{0:T(512)(128)(4,1)S(1)} %copy-done.27, pred[512]{0:T(512)(128)(4,1)S(1)} %copy-done.26), kind=kLoop, calls=%fused_computation.6 | loop fusion | flops 193536 | bytes 1162240 | tf_op jit(solution)/shard_map/jit(_where)/select_n | solution.py:182
  173.2 3.4 %fusion.16 = f32[9,21,4,128]{3,1,2,0:T(8,128)S(1)} fusion(f32[9,21,4,128,1]{1,0,3,2,4:T(8,128)S(1)} %bitcast.275, f32[3,4,128]{2,0,1:T(4,128)S(1)} %fusion.164, f32[3,21,21]{2,1,0:T(8,128)S(1)} %copy-done.7), kind=kOutput, calls=%fused_computation.18 | convolution fusion | flops 73640448 | bytes 785580 | tf_op jit(solution)/shard_map/hil,qlfe->hqife/dot_general | solution.py:104
  (296 shorter events, 43.5 us)
Async XLA Ops:
  1.5 16.7 %copy-start.29 = (pred[192]{0:T(512)(128)(4,1)}, pred[192]{0:T(512)(128)(4,1)S(1)}, u32[]{:S(2)}) copy-start(pred[192]{0:T(512)(128)(4,1)S(1)} %compare_and_fusion) | copy-start | bytes 580
  2.9 15.3 %copy-start.21 = (f32[192]{0:T(256)}, f32[192]{0:T(256)S(1)}, u32[]{:S(2)}) copy-start(f32[192]{0:T(256)S(1)} %reshape.1889) | copy-start | bytes 2308
  3.8 25.1 %copy-start.8 = (f32[3,128]{1,0:T(4,128)}, f32[3,128]{1,0:T(4,128)S(1)}, u32[]{:S(2)}) copy-start(f32[3,128]{1,0:T(4,128)S(1)} %get-tuple-element.103) | copy-start | bytes 4612
  18.3 9.9 %copy-start.10 = (f32[4,3,128]{2,0,1:T(4,128)S(1)}, f32[4,3,128]{2,0,1:T(4,128)}, u32[]{:S(2)}) copy-start(f32[4,3,128]{2,0,1:T(4,128)} %param.28) | copy-start | bytes 18436
  18.3 10.5 %copy-start.28 = (s32[1,1,8,24]{3,2,1,0:T(8,128)S(1)}, s32[1,1,8,24]{3,2,1,0:T(8,128)}, u32[]{:S(2)}) copy-start(s32[1,1,8,24]{3,2,1,0:T(8,128)} %param.33) | copy-start | bytes 2308
  18.3 10.6 %copy-start.31 = (s32[4,128]{1,0:T(4,128)S(1)}, s32[4,128]{1,0:T(4,128)}, u32[]{:S(2)}) copy-start(s32[4,128]{1,0:T(4,128)} %param.29) | copy-start | bytes 6148
  18.3 10.6 %copy-start.2 = (f32[3,56,56]{2,1,0:T(8,128)S(1)}, f32[3,56,56]{2,1,0:T(8,128)}, u32[]{:S(2)}) copy-start(f32[3,56,56]{2,1,0:T(8,128)} %param.21) | copy-start | bytes 112900
  19.5 10.4 %copy-start.33 = (f32[128]{0:T(128)S(1)}, f32[128]{0:T(128)}, u32[]{:S(2)}) copy-start(f32[128]{0:T(128)} %get-tuple-element.97) | copy-start | bytes 1540
  19.5 11.5 %copy-start.19 = (s32[1024]{0:T(1024)S(1)}, s32[1024]{0:T(1024)}, u32[]{:S(2)}) copy-start(s32[1024]{0:T(1024)} %get-tuple-element.105) | copy-start | bytes 12292
  20.1 16.4 %collective-permute-start = (f32[9,21,3,24]{3,1,2,0:T(8,128)S(1)}, f32[9,21,3,24]{3,1,2,0:T(8,128)S(1)}, u32[]{:S(2)}, u32[]{:S(2)}) collective-permute-start(f32[9,21,3,24]{3,1,2,0:T(8,128)S(1)} %pad_maximum_fusion), channel_id=1, source_target_pairs={{0,1},{1,2},{2,3},{3,4},{4,5},{5,6},{6,7},{8,9},{9,10},{10,11},{11... | collective-permute-start | bytes 163304 | tf_op jit(solution)/shard_map/ppermute | solution.py:44
  25.7 11.7 %collective-permute-start.1 = (f32[9,21,3,24]{3,1,2,0:T(8,128)}, f32[9,21,3,24]{3,1,2,0:T(8,128)}, u32[]{:S(2)}, u32[]{:S(2)}) collective-permute-start(f32[9,21,3,24]{3,1,2,0:T(8,128)} %pad_maximum_fusion.1), channel_id=1, source_target_pairs={{1,0},{2,1},{3,2},{4,3},{5,4},{6,5},{7,6},{9,8},{10,9},{11,10},{12... | collective-permute-start | bytes 163304 | tf_op jit(solution)/shard_map/ppermute | solution.py:44
  38.6 10.9 %collective-permute-start.2 = (f32[9,21,3,24]{3,1,2,0:T(8,128)S(1)}, f32[9,21,3,24]{3,1,2,0:T(8,128)S(1)}, u32[]{:S(2)}, u32[]{:S(2)}) collective-permute-start(f32[9,21,3,24]{3,1,2,0:T(8,128)S(1)} %pad_maximum_fusion.2), channel_id=1, source_target_pairs={{0,8},{8,16},{16,24},{24,32},{32,40},{40,48},{48,56},{56,64},{64,7... | collective-permute-start | bytes 163304 | tf_op jit(solution)/shard_map/ppermute | solution.py:44
  45.7 11.8 %collective-permute-start.3 = (f32[9,21,3,24]{3,1,2,0:T(8,128)S(1)}, f32[9,21,3,24]{3,1,2,0:T(8,128)S(1)}, u32[]{:S(2)}, u32[]{:S(2)}) collective-permute-start(f32[9,21,3,24]{3,1,2,0:T(8,128)S(1)} %pad_maximum_fusion.3), channel_id=1, source_target_pairs={{8,0},{16,8},{24,16},{32,24},{40,32},{48,40},{56,48},{64,56},{72,6... | collective-permute-start | bytes 163304 | tf_op jit(solution)/shard_map/ppermute | solution.py:44
  83.1 9.2 %copy-start.15 = (f32[4,128]{1,0:T(4,128)S(1)}, f32[4,128]{1,0:T(4,128)}, u32[]{:S(2)}) copy-start(f32[4,128]{1,0:T(4,128)} %get-tuple-element.92) | copy-start | bytes 6148
  83.1 9.2 %copy-start.17 = (f32[4,128]{1,0:T(4,128)S(1)}, f32[4,128]{1,0:T(4,128)}, u32[]{:S(2)}) copy-start(f32[4,128]{1,0:T(4,128)} %get-tuple-element.93) | copy-start | bytes 6148
  108.3 10.9 %collective-permute-start.4 = (f32[9,21,3,24]{3,1,2,0:T(8,128)S(1)}, f32[9,21,3,24]{3,1,2,0:T(8,128)S(1)}, u32[]{:S(2)}, u32[]{:S(2)}) collective-permute-start(f32[9,21,3,24]{3,1,2,0:T(8,128)S(1)} %pad_maximum_fusion.4), channel_id=1, source_target_pairs={{0,1},{1,2},{2,3},{3,4},{4,5},{5,6},{6,7},{8,9},{9,10},{10,11},{11... | collective-permute-start | bytes 163304 | tf_op jit(solution)/shard_map/ppermute | solution.py:44
  116.7 9.1 %collective-permute-start.5 = (f32[9,21,3,24]{3,1,2,0:T(8,128)S(1)}, f32[9,21,3,24]{3,1,2,0:T(8,128)S(1)}, u32[]{:S(2)}, u32[]{:S(2)}) collective-permute-start(f32[9,21,3,24]{3,1,2,0:T(8,128)S(1)} %pad_maximum_fusion.5), channel_id=1, source_target_pairs={{1,0},{2,1},{3,2},{4,3},{5,4},{6,5},{7,6},{9,8},{10,9},{11,10},{12... | collective-permute-start | bytes 163304 | tf_op jit(solution)/shard_map/ppermute | solution.py:44
  125.9 8.0 %collective-permute-start.6 = (f32[9,21,3,24]{3,1,2,0:T(8,128)S(1)}, f32[9,21,3,24]{3,1,2,0:T(8,128)S(1)}, u32[]{:S(2)}, u32[]{:S(2)}) collective-permute-start(f32[9,21,3,24]{3,1,2,0:T(8,128)S(1)} %pad_maximum_fusion.6), channel_id=1, source_target_pairs={{0,8},{8,16},{16,24},{24,32},{32,40},{40,48},{48,56},{56,64},{64,7... | collective-permute-start | bytes 163304 | tf_op jit(solution)/shard_map/ppermute | solution.py:44
  130.1 11.8 %collective-permute-start.7 = (f32[9,21,3,24]{3,1,2,0:T(8,128)S(1)}, f32[9,21,3,24]{3,1,2,0:T(8,128)S(1)}, u32[]{:S(2)}, u32[]{:S(2)}) collective-permute-start(f32[9,21,3,24]{3,1,2,0:T(8,128)S(1)} %pad_maximum_fusion.7), channel_id=1, source_target_pairs={{8,0},{16,8},{24,16},{32,24},{40,32},{48,40},{56,48},{64,56},{72,6... | collective-permute-start | bytes 163304 | tf_op jit(solution)/shard_map/ppermute | solution.py:44
  142.2 25.2 %copy-start.26 = (pred[512]{0:T(512)(128)(4,1)S(1)}, pred[512]{0:T(512)(128)(4,1)}, u32[]{:S(2)}) copy-start(pred[512]{0:T(512)(128)(4,1)} %compare_bitcast_fusion) | copy-start | bytes 1540
  142.2 25.1 %copy-start.27 = (pred[512]{0:T(512)(128)(4,1)S(1)}, pred[512]{0:T(512)(128)(4,1)}, u32[]{:S(2)}) copy-start(pred[512]{0:T(512)(128)(4,1)} %get-tuple-element.43) | copy-start | bytes 1540
  167.4 9.3 %copy-start.14 = (f32[4,128]{1,0:T(4,128)S(1)}, f32[4,128]{1,0:T(4,128)}, u32[]{:S(2)}) copy-start(f32[4,128]{1,0:T(4,128)} %get-tuple-element.91) | copy-start | bytes 6148
  167.4 9.3 %copy-start.16 = (f32[4,128]{1,0:T(4,128)S(1)}, f32[4,128]{1,0:T(4,128)}, u32[]{:S(2)}) copy-start(f32[4,128]{1,0:T(4,128)} %get-tuple-element.92) | copy-start | bytes 6148
  167.4 9.3 %copy-start.18 = (f32[4,128]{1,0:T(4,128)S(1)}, f32[4,128]{1,0:T(4,128)}, u32[]{:S(2)}) copy-start(f32[4,128]{1,0:T(4,128)} %get-tuple-element.93) | copy-start | bytes 6148
  (18 other events, 84.7 us)
where the time goes:
time: 181 us; the launch traced here: 178 us
  local copies, waits for them, and re-layouts  80 us (44%)
  starting transfers between devices  26.7 us (15%)
  waiting for transfers between devices  26.3 us (15%)
  matrix products  21.9 us (12%)
  other arithmetic  21.7 us (12%)
    scatter x2, local copies, waits for them, and re-layouts, per_device(): jnp.zeros_like(flat_faces).at[:, :, targets].set(received, mode='drop')  41.8 us
    ppermute x8, starting transfers between devices, shifted(): return lax.ppermute(x, axis, pairs)  26.7 us
    ppermute x8, waiting for transfers between devices, shifted(): return lax.ppermute(x, axis, pairs)  26.3 us
    select_n x2, other arithmetic, per_device(): jnp.where(inside, local_data, arrived).reshape(9, face_width, 4, elem_count)  11.5 us
    gather x2, local copies, waits for them, and re-layouts, per_device(): local_data = jnp.take(flat_faces, local_index, axis=2)  10.2 us
    dot_general x10, matrix products, predict(): jnp.einsum('dab,qbe->dqae', grad_matrix, derivative, precision=exact_mode)  9.66 us
    dot_general x2, matrix products, face_update(): jnp.einsum('hil,qlfe->hqife', rotate, neighbour_data, precision=exact_mode)  6.9 us
    gather x2, local copies, waits for them, and re-layouts, per_device(): jnp.take(flat_faces, source_index, axis=2) * source_mask  5.91 us
  transfers between devices with their start and end apart: 8, of which 6 were waited for; matrix products, arithmetic and copies ran while one was open for 9% of the time, Pallas kernels for 0%

commit v1 on v0

v1 whole, which is shorter than its diff:
```python
import functools

import jax
import jax.numpy as jnp
from jax import lax
from jax.experimental import pallas as pl
from jax.experimental.pallas import tpu as pltpu
from jax.sharding import PartitionSpec as P

ORDER = 6
STEPS = 2
TIME_STEP = 0.8
OFFSETS = ((-1, -1), (-1, 0), (-1, 1), (0, -1), (0, 1), (1, -1), (1, 0), (1, 1))
MESH = pl.DeviceIdType.MESH
F32 = jnp.float32
BF16 = jnp.bfloat16
QUANT = 9
BASIS = 56
KBLOCK = 64
FACE = 21
FROWS = 24
ELEMS = 128
FACES = 4 * ELEMS
SLOTS = 24
WIDE = 256


def dot(a, b):
    return lax.dot_general(a, b, (((1,), (0,)), ((), ())), preferred_element_type=F32)


def dot_nt(a, b):
    return lax.dot_general(a, b, (((1,), (1,)), ((), ())), preferred_element_type=F32)


def low_of(x):
    return x - x.astype(BF16).astype(F32)


def widen(x, rows):
    if x.shape[0] == rows:
        return x
    return jnp.concatenate([x, jnp.zeros((rows - x.shape[0], x.shape[1]), F32)], axis=0)


def stacked(slabs, rows):
    columns = []
    for slab in slabs:
        full = widen(slab, rows)
        high = full.astype(BF16)
        low = (full - high.astype(F32)).astype(BF16)
        columns.append(jnp.concatenate([high, high, low], axis=0))
    return jnp.concatenate(columns, axis=1)


def stress_rates(ux, vy, wz, uv, vw, uw, lame, shear2, shear):
    spread = lame * (ux + vy + wz)
    return [
        spread + shear2 * ux,
        spread + shear2 * vy,
        spread + shear2 * wz,
        shear * uv,
        shear * vw,
        shear * uw,
    ]


def kernel(
    rows,
    cols,
    dof_ref,
    grad_ref,
    stiff_ref,
    proj_ref,
    lift_ref,
    rot_ref,
    mat_ref,
    mid_ref,
    jac_ref,
    nrm_ref,
    ori_ref,
    near_ref,
    near_face_ref,
    send_list_ref,
    recv_list_ref,
    out_ref,
    tmp,
    grad_w,
    stiff_w,
    proj_w,
    lift_w,
    rot_w,
    near_w,
    give_w,
    take_w,
    send_buf,
    recv_buf,
    send_sem,
    recv_sem,
):
    row = lax.axis_index("prow")
    col = lax.axis_index("pcol")
    partners = [
        (lax.rem(row + (dr + rows), rows), lax.rem(col + (dc + cols), cols)) for dr, dc in OFFSETS
    ]
    barrier = pltpu.get_barrier_semaphore()
    for partner in partners:
        pl.semaphore_signal(barrier, inc=1, device_id=partner, device_id_type=MESH)

    def split_store(dest, at, block, step_k, first=True):
        height, width = block.shape
        dest[at : at + height, 0:width] = block
        dest[at : at + height, step_k : step_k + width] = low_of(block)
        dest[at : at + height, 2 * step_k : 2 * step_k + width] = block

    tmp[...] = jnp.zeros_like(tmp)
    for d in range(3):
        split_store(tmp, d * BASIS, grad_ref[d], KBLOCK)
    grad_w[...] = tmp[0:176, 0 : 3 * KBLOCK].astype(BF16)
    for d in range(3):
        split_store(tmp, d * BASIS, stiff_ref[d], KBLOCK)
    stiff_w[...] = tmp[0:176, 0 : 3 * KBLOCK].astype(BF16)
    tmp[...] = jnp.zeros_like(tmp)
    for f in range(4):
        split_store(tmp, f * FROWS, proj_ref[f], KBLOCK)
    proj_w[...] = tmp[0:96, 0 : 3 * KBLOCK].astype(BF16)
    tmp[...] = jnp.zeros_like(tmp)
    for h in range(3):
        split_store(tmp, h * FROWS, rot_ref[h], FROWS)
    rot_w[...] = tmp[0:80, 0:80].astype(BF16)
    tmp[...] = jnp.zeros_like(tmp)
    for f in range(4):
        block = lift_ref[f]
        tmp[0:BASIS, f * FROWS : f * FROWS + FACE] = block
        tmp[0:BASIS, 96 + f * FROWS : 96 + f * FROWS + FACE] = low_of(block)
        tmp[0:BASIS, 192 + f * FROWS : 192 + f * FROWS + FACE] = block
    lift_w[...] = tmp[0:64, 0:288].astype(BF16)

    face_rows = lax.broadcasted_iota(jnp.int32, (FACES, ELEMS), 0)
    for f in range(4):
        near = near_ref[f : f + 1, :]
        source = jnp.where(near >= 0, near_face_ref[f : f + 1, :] * ELEMS + near, -1)
        near_w[:, f * ELEMS : (f + 1) * ELEMS] = (face_rows == source).astype(F32).astype(BF16)
    outside = jnp.concatenate([near_ref[f : f + 1, :] < 0 for f in range(4)], axis=1)
    face_ids = lax.broadcasted_iota(jnp.int32, (SLOTS, FACES), 1)
    give_ids = jnp.transpose(send_list_ref[0, 0])
    take_ids = jnp.transpose(recv_list_ref[0, 0])
    give_parts = []
    take_parts = []
    for d in range(8):
        give_parts.append((give_ids[:, d : d + 1] == face_ids).astype(F32))
        take_parts.append(
            jnp.where((take_ids[:, d : d + 1] == face_ids) & outside, 1.0, 0.0).astype(F32)
        )
    give_w[...] = jnp.concatenate(give_parts, axis=0).astype(BF16)
    take_w[...] = jnp.concatenate(take_parts, axis=0).astype(BF16)

    hot = lax.broadcasted_iota(jnp.int32, (16, ELEMS), 0) == mid_ref[...]
    density, lame, shear = [
        jnp.sum(jnp.where(hot, mat_ref[:, j : j + 1], 0.0), axis=0, keepdims=True) for j in range(3)
    ]
    inverse = 1.0 / density
    jac = [[jac_ref[d, k : k + 1, :] for k in range(3)] for d in range(3)]
    root = jnp.sqrt((lame + 2.0 * shear) * inverse)
    orient = jnp.concatenate([ori_ref[f : f + 1, :] for f in range(4)], axis=1)

    def along(slopes, columns):
        def one(place, k):
            parts = [
                jac[d][k]
                * slopes[d * BASIS : (d + 1) * BASIS, place * ELEMS : (place + 1) * ELEMS]
                for d in range(3)
            ]
            return parts[0] + parts[1] + parts[2]

        return one

    def stress_from(slopes, scale):
        one = along(slopes, 3)
        ux, vy, wz = one(0, 0), one(1, 1), one(2, 2)
        uv = one(1, 0) + one(0, 1)
        vw = one(2, 1) + one(1, 2)
        uw = one(2, 0) + one(0, 2)
        return stress_rates(
            ux, vy, wz, uv, vw, uw, scale * lame, (2.0 * scale) * shear, scale * shear
        )

    def speed_from(slopes, scale):
        one = along(slopes, 6)
        over = scale * inverse
        return [
            over * (one(0, 0) + one(3, 1) + one(5, 2)),
            over * (one(3, 0) + one(1, 1) + one(4, 2)),
            over * (one(5, 0) + one(4, 1) + one(2, 2)),
        ]

    for step in range(STEPS):
        current = dof_ref if step == 0 else out_ref
        level = [TIME_STEP * current[q] for q in range(QUANT)]
        total = list(level)
        for power in range(1, ORDER):
            scale = TIME_STEP / (power + 1)
            from_stress = dot(grad_w[...], stacked(level[:6], KBLOCK))
            from_speed = dot(grad_w[...], stacked(level[6:], KBLOCK))
            level = stress_from(from_speed, scale) + speed_from(from_stress, scale)
            total = [t + x for t, x in zip(total, level)]

        whole = stacked(total, KBLOCK)
        own = dot(proj_w[...], whole)
        faces = jnp.concatenate(
            [
                jnp.concatenate(
                    [
                        own[f * FROWS : (f + 1) * FROWS, q * ELEMS : (q + 1) * ELEMS]
                        for f in range(4)
                    ],
                    axis=1,
                )
                for q in range(QUANT)
            ]
            + [jnp.zeros((WIDE - QUANT * FROWS, FACES), F32)],
            axis=0,
        )
        faces_high = faces.astype(BF16)
        faces_low = (faces - faces_high.astype(F32)).astype(BF16)
        outgoing = dot_nt(give_w[...], faces_high) + dot_nt(give_w[...], faces_low)
        for d in range(8):
            send_buf[step, d] = outgoing[d * SLOTS : (d + 1) * SLOTS]
        if step == 0:
            pl.semaphore_wait(barrier, 8)
        copies = []
        for d in range(8):
            copy = pltpu.make_async_remote_copy(
                src_ref=send_buf.at[step, d],
                dst_ref=recv_buf.at[step, 7 - d],
                send_sem=send_sem.at[step, d],
                recv_sem=recv_sem.at[step, 7 - d],
                device_id=partners[d],
                device_id_type=MESH,
            )
            copy.start()
            copies.append(copy)

        slopes = dot(stiff_w[...], whole)
        volume = stress_from(slopes[:, 6 * ELEMS :], -1.0) + speed_from(slopes[:, : 6 * ELEMS], -1.0)
        for q in range(QUANT):
            out_ref[q] = current[q] + volume[q]
        beside = dot(faces_high, near_w[...]) + dot(faces_low, near_w[...])

        for copy in copies:
            copy.wait_recv()
        got = jnp.transpose(
            jnp.concatenate([recv_buf[step, d] for d in range(8)], axis=0)
        )
        got_high = got.astype(BF16)
        got_low = (got - got_high.astype(F32)).astype(BF16)
        beside = beside + dot(got_high, take_w[...]) + dot(got_low, take_w[...])

        turned = []
        for q in range(QUANT):
            block = beside[q * FROWS : (q + 1) * FROWS]
            low = low_of(block)
            right = jnp.concatenate([block, block, low, jnp.zeros((8, FACES), F32)], axis=0)
            each = dot(rot_w[...], right.astype(BF16))
            turned.append(
                jnp.where(
                    orient == 0,
                    each[0:FROWS],
                    jnp.where(orient == 1, each[FROWS : 2 * FROWS], each[2 * FROWS : 3 * FROWS]),
                )
            )

        fluxes = [[] for _ in range(QUANT)]
        for f in range(4):
            here = slice(f * ELEMS, (f + 1) * ELEMS)
            n = [nrm_ref[f, k : k + 1, :] for k in range(3)]
            both = []
            apart = []
            for q in range(QUANT):
                mine = own[f * FROWS : (f + 1) * FROWS, q * ELEMS : (q + 1) * ELEMS]
                theirs = turned[q][:, here]
                both.append(mine + theirs)
                apart.append(mine - theirs)
            half = 0.5 * root * (jnp.abs(n[0]) + jnp.abs(n[1]) + jnp.abs(n[2]))
            u, v, w = both[6:]
            ns = [-0.5 * shear * x for x in n]
            spread = (-0.5 * lame) * (n[0] * u + n[1] * v + n[2] * w)
            over = [-0.5 * inverse * x for x in n]
            xx, yy, zz, xy, yz, xz = both[:6]
            flux = [
                spread + (2.0 * ns[0]) * u,
                spread + (2.0 * ns[1]) * v,
                spread + (2.0 * ns[2]) * w,
                ns[0] * v + ns[1] * u,
                ns[1] * w + ns[2] * v,
                ns[0] * w + ns[2] * u,
                over[0] * xx + over[1] * xy + over[2] * xz,
                over[0] * xy + over[1] * yy + over[2] * yz,
                over[0] * xz + over[1] * yz + over[2] * zz,
            ]
            for q in range(QUANT):
                fluxes[q].append(flux[q] + half * apart[q])
        lifted = dot(
            lift_w[...], stacked([jnp.concatenate(parts, axis=0) for parts in fluxes], 96)
        )
        for q in range(QUANT):
            out_ref[q] = out_ref[q] - lifted[0:BASIS, q * ELEMS : (q + 1) * ELEMS]
        for copy in copies:
            copy.wait_send()


def solution(mesh):
    rows, cols = mesh.shape["prow"], mesh.shape["pcol"]

    def per_device(*args):
        args = list(args)
        args[7] = args[7].reshape(1, ELEMS)
        vmem = pl.BlockSpec(memory_space=pltpu.VMEM)
        return pl.pallas_call(
            functools.partial(kernel, rows, cols),
            out_shape=jax.ShapeDtypeStruct((QUANT, BASIS, ELEMS), F32),
            in_specs=[vmem] * 15,
            out_specs=vmem,
            scratch_shapes=[
                pltpu.VMEM((176, 384), F32),
                pltpu.VMEM((176, 3 * KBLOCK), BF16),
                pltpu.VMEM((176, 3 * KBLOCK), BF16),
                pltpu.VMEM((96, 3 * KBLOCK), BF16),
                pltpu.VMEM((64, 288), BF16),
                pltpu.VMEM((80, 80), BF16),
                pltpu.VMEM((FACES, FACES), BF16),
                pltpu.VMEM((8 * SLOTS, FACES), BF16),
                pltpu.VMEM((8 * SLOTS, FACES), BF16),
                pltpu.VMEM((STEPS, 8, SLOTS, WIDE), F32),
                pltpu.VMEM((STEPS, 8, SLOTS, WIDE), F32),
                pltpu.SemaphoreType.DMA((STEPS, 8)),
                pltpu.SemaphoreType.DMA((STEPS, 8)),
            ],
            compiler_params=pltpu.CompilerParams(
                collective_id=0, has_side_effects=True, vmem_limit_bytes=40 * 1024 * 1024
            ),
        )(*args)

    both = ("prow", "pcol")
    return jax.shard_map(
        per_device,
        mesh=mesh,
        in_specs=(
            P(None, None, both),
            P(),
            P(),
            P(),
            P(),
            P(),
            P(),
            P(both),
            P(None, None, both),
            P(None, None, both),
            P(None, both),
            P(None, both),
            P(None, both),
            P("prow", "pcol", None, None),
            P("prow", "pcol", None, None),
        ),
        out_specs=P(None, None, both),
        check_vma=False,
    )
```

time: 181 us -> 40.8 us (0.23)
  the two profiles are of different devices: /device:TPU:223 before, /device:TPU:24 now
where the time goes in v1:
time: 40.8 us; the launch traced here: 40.4 us
  Pallas kernels  32.4 us (79%)
  local copies, waits for them, and re-layouts  7.83 us (19%)
    pallas_call x1, Pallas kernels, per_device(): pl.pallas_call(functools.partial(kernel, rows, cols), out_shape=jax.Shape...  32.4 us
    unnamed x27, local copies, waits for them, and re-layouts  7.83 us

profile of v1, /device:TPU:24, one launch (start us, length us, event | category | flops | bytes accessed | tf_op | source)
XLA Modules:
  0.0 40.4 jit_solution(8338734238021889843)
XLA Ops:
  0.0 0.0 copy-start
  0.0 0.8 %copy.18.mat_ref = f32[16,3]{1,0:T(8,128)S(1)} copy(f32[16,3]{0,1:T(4,128)} %param.21) | data formatting | bytes 384 | tf_op args[6]
  0.8 0.7 %copy.19.nrm_ref = f32[4,3,128]{2,1,0:T(4,128)S(1)} copy(f32[4,3,128]{2,0,1:T(4,128)} %param.24) | data formatting | bytes 12288 | tf_op args[9]
  1.5 0.8 %copy.16.proj_ref = f32[4,21,56]{2,1,0:T(8,128)S(1)} copy(f32[4,21,56]{2,0,1:T(4,128)} %param.18) | data formatting | bytes 37632 | tf_op args[3]
  2.3 0.0 copy-start.4
  2.3 0.0 copy-start.6
  2.3 0.0 copy-start.7
  2.3 0.0 copy-start.10
  2.3 0.9 %copy.17.lift_ref = f32[4,56,21]{2,1,0:T(8,128)S(1)} copy(f32[4,56,21]{1,0,2:T(4,128)} %param.19) | data formatting | bytes 37632 | tf_op args[4]
  3.2 0.0 copy-done
  3.3 0.0 copy-done.4
  3.3 0.0 copy-done.5
  3.3 0.0 copy-done.6
  3.3 0.0 copy-done.7
  3.3 0.0 copy-done.10
  3.3 0.0 copy-start.1
  3.3 0.9 %copy-done.1 = f32[3,56,56]{2,1,0:T(8,128)S(1)} copy-done((f32[3,56,56]{2,1,0:T(8,128)S(1)}, f32[3,56,56]{2,1,0:T(8,128)}, u32[]{:S(2)}) %copy-start.1) | copy-done | bytes 37656
  4.2 0.0 copy-start.2
  4.2 0.9 %copy-done.2 = f32[3,56,56]{2,1,0:T(8,128)S(1)} copy-done((f32[3,56,56]{2,1,0:T(8,128)S(1)}, f32[3,56,56]{2,1,0:T(8,128)}, u32[]{:S(2)}) %copy-start.2) | copy-done | bytes 37656
  5.1 0.8 %copy-done.3 = f32[3,21,21]{2,1,0:T(8,128)S(1)} copy-done((f32[3,21,21]{2,1,0:T(8,128)S(1)}, f32[3,21,21]{2,1,0:T(8,128)}, u32[]{:S(2)}) %copy-start.3) | copy-done | bytes 5316
  5.9 0.7 %copy-done.8 = s32[4,128]{1,0:T(4,128)S(1)} copy-done((s32[4,128]{1,0:T(4,128)S(1)}, s32[4,128]{1,0:T(4,128)}, u32[]{:S(2)}) %copy-start.8) | copy-done | bytes 2072
  6.5 0.7 %copy-done.9 = s32[4,128]{1,0:T(4,128)S(1)} copy-done((s32[4,128]{1,0:T(4,128)S(1)}, s32[4,128]{1,0:T(4,128)}, u32[]{:S(2)}) %copy-start.9) | copy-done | bytes 2072
  7.2 32.4 %shard_map.145 = f32[9,56,128]{2,1,0:T(8,128)S(1)} custom-call(f32[9,56,128]{2,1,0:T(8,128)S(1)} %copy-done, f32[3,56,56]{2,1,0:T(8,128)S(1)} %copy-done.1, f32[3,56,56]{2,1,0:T(8,128)S(1)} %copy-done.2, f32[4,21,56]{2,1,0:T(8,128)S(1)} %copy.16.proj_ref, f32[4,56,21]{2,1,0:T(8,128)S(1)} %copy.17.lift_ref, f32[3,21,21]{2,1,0:T(8,128)S(1)} %copy-done.3, ...), custom_call_target="tpu_custom_call" | custom-call | tf_op jit(solution)/shard_map/pallas_call | solution.py:319
  39.7 0.7 %copy.21 = f32[9,56,128]{2,1,0:T(8,128)} copy(f32[9,56,128]{2,1,0:T(8,128)S(1)} %shard_map.145) | data formatting | bytes 516096
  (4 shorter events, 0.0 us)
Async XLA Ops:
  0.0 3.3 %copy-start = (f32[9,56,128]{2,1,0:T(8,128)S(1)}, f32[9,56,128]{2,1,0:T(8,128)}, u32[]{:S(2)}) copy-start(f32[9,56,128]{2,1,0:T(8,128)} %dof_ref.1) | copy-start | bytes 774148
  2.3 1.0 %copy-start.4 = (f32[3,3,128]{2,1,0:T(4,128)S(1)}, f32[3,3,128]{2,1,0:T(4,128)}, u32[]{:S(2)}) copy-start(f32[3,3,128]{2,1,0:T(4,128)} %jac_ref.1) | copy-start | bytes 13828
  2.3 1.0 %copy-start.5 = (s32[1,1,8,24]{3,2,1,0:T(8,128)S(1)}, s32[1,1,8,24]{3,2,1,0:T(8,128)}, u32[]{:S(2)}) copy-start(s32[1,1,8,24]{3,2,1,0:T(8,128)} %send_list_ref.1) | copy-start | bytes 2308
  2.3 1.0 %copy-start.6 = (s32[1,1,8,24]{3,2,1,0:T(8,128)S(1)}, s32[1,1,8,24]{3,2,1,0:T(8,128)}, u32[]{:S(2)}) copy-start(s32[1,1,8,24]{3,2,1,0:T(8,128)} %recv_list_ref.1) | copy-start | bytes 2308
  2.3 1.0 %copy-start.7 = (s32[4,128]{1,0:T(4,128)S(1)}, s32[4,128]{1,0:T(4,128)}, u32[]{:S(2)}) copy-start(s32[4,128]{1,0:T(4,128)} %ori_ref.1) | copy-start | bytes 6148
  2.3 1.0 %copy-start.10 = (s32[128]{0:T(128)S(1)}, s32[128]{0:T(128)}, u32[]{:S(2)}) copy-start(s32[128]{0:T(128)} %param.22) | copy-start | bytes 1540
  3.3 0.9 %copy-start.1 = (f32[3,56,56]{2,1,0:T(8,128)S(1)}, f32[3,56,56]{2,1,0:T(8,128)}, u32[]{:S(2)}) copy-start(f32[3,56,56]{2,1,0:T(8,128)} %grad_ref.1) | copy-start | bytes 112900
  4.2 0.9 %copy-start.2 = (f32[3,56,56]{2,1,0:T(8,128)S(1)}, f32[3,56,56]{2,1,0:T(8,128)}, u32[]{:S(2)}) copy-start(f32[3,56,56]{2,1,0:T(8,128)} %stiff_ref.1) | copy-start | bytes 112900
  5.1 0.8 %copy-start.3 = (f32[3,21,21]{2,1,0:T(8,128)S(1)}, f32[3,21,21]{2,1,0:T(8,128)}, u32[]{:S(2)}) copy-start(f32[3,21,21]{2,1,0:T(8,128)} %rot_ref.1) | copy-start | bytes 15880
  5.9 0.7 %copy-start.8 = (s32[4,128]{1,0:T(4,128)S(1)}, s32[4,128]{1,0:T(4,128)}, u32[]{:S(2)}) copy-start(s32[4,128]{1,0:T(4,128)} %near_ref.1) | copy-start | bytes 6148
  6.5 0.7 %copy-start.9 = (s32[4,128]{1,0:T(4,128)S(1)}, s32[4,128]{1,0:T(4,128)}, u32[]{:S(2)}) copy-start(s32[4,128]{1,0:T(4,128)} %near_face_ref.1) | copy-start | bytes 6148

commit v2 on v1

--- a/solution.py
+++ b/solution.py
@@ -68,6 +68,22 @@
 def kernel(
     rows,
     cols,
+    dof_hbm,
+    grad_hbm,
+    stiff_hbm,
+    proj_hbm,
+    lift_hbm,
+    rot_hbm,
+    mat_hbm,
+    mid_hbm,
+    jac_hbm,
+    nrm_hbm,
+    ori_hbm,
+    near_hbm,
+    near_face_hbm,
+    send_list_hbm,
+    recv_list_hbm,
+    out_ref,
     dof_ref,
     grad_ref,
     stiff_ref,
@@ -83,7 +99,7 @@
     near_face_ref,
     send_list_ref,
     recv_list_ref,
-    out_ref,
+    load_sem,
     tmp,
     grad_w,
     stiff_w,
@@ -98,14 +114,61 @@
     send_sem,
     recv_sem,
 ):
+    loads = []
+    for at, (source, dest) in enumerate(
+        [
+            (grad_hbm, grad_ref),
+            (dof_hbm, dof_ref),
+            (jac_hbm, jac_ref),
+            (mat_hbm, mat_ref),
+            (mid_hbm, mid_ref),
+            (proj_hbm, proj_ref),
+            (send_list_hbm, send_list_ref),
+            (stiff_hbm, stiff_ref),
+            (lift_hbm, lift_ref),
+            (rot_hbm, rot_ref),
+            (nrm_hbm, nrm_ref),
+            (ori_hbm, ori_ref),
+            (near_hbm, near_ref),
+            (near_face_hbm, near_face_ref),
+            (recv_list_hbm, recv_list_ref),
+        ]
+    ):
+        load = pltpu.make_async_copy(source, dest, load_sem.at[at])
+        load.start()
+        loads.append(load)
+
     row = lax.axis_index("prow")
     col = lax.axis_index("pcol")
-    partners = [
-        (lax.rem(row + (dr + rows), rows), lax.rem(col + (dc + cols), cols)) for dr, dc in OFFSETS
-    ]
+    partners = []
+    exists = []
+    for dr, dc in OFFSETS:
+        there = [row + dr, col + dc]
+        inside = []
+        if dr:
+            inside.append(there[0] >= 0 if dr < 0 else there[0] < rows)
+        if dc:
+            inside.append(there[1] >= 0 if dc < 0 else there[1] < cols)
+        partners.append((there[0], there[1]))
+        exists.append(functools.reduce(jnp.logical_and, inside))
+    up_down = (row > 0).astype(jnp.int32) + (row < rows - 1).astype(jnp.int32)
+    left_right = (col > 0).astype(jnp.int32) + (col < cols - 1).astype(jnp.int32)
+    peers = up_down + left_right + up_down * left_right
     barrier = pltpu.get_barrier_semaphore()
-    for partner in partners:
-        pl.semaphore_signal(barrier, inc=1, device_id=partner, device_id_type=MESH)
+    for d in range(8):
+
+        @pl.when(exists[d])
+        def _(d=d):
+            pl.semaphore_signal(barrier, inc=1, device_id=partners[d], device_id_type=MESH)
+
+        @pl.when(jnp.logical_not(exists[d]))
+        def _(d=d):
+            for step in range(STEPS):
+                recv_buf[step, d] = jnp.zeros((SLOTS, WIDE), F32)
+
+    tmp[...] = jnp.zeros_like(tmp)
+    for load in loads:
+        load.wait()
 
     def split_store(dest, at, block, step_k, first=True):
         height, width = block.shape
@@ -113,7 +176,6 @@
         dest[at : at + height, step_k : step_k + width] = low_of(block)
         dest[at : at + height, 2 * step_k : 2 * step_k + width] = block
 
-    tmp[...] = jnp.zeros_like(tmp)
     for d in range(3):
         split_store(tmp, d * BASIS, grad_ref[d], KBLOCK)
     grad_w[...] = tmp[0:176, 0 : 3 * KBLOCK].astype(BF16)
@@ -122,7 +184,9 @@
     stiff_w[...] = tmp[0:176, 0 : 3 * KBLOCK].astype(BF16)
     tmp[...] = jnp.zeros_like(tmp)
     for f in range(4):
-        split_store(tmp, f * FROWS, proj_ref[f], KBLOCK)
+        for i in range(FACE):
+            tmp[f * FROWS + i : f * FROWS + i + 1, 0:BASIS] = proj_ref[i, f : f + 1, :]
+    split_store(tmp, 0, tmp[0:96, 0:KBLOCK], KBLOCK)
     proj_w[...] = tmp[0:96, 0 : 3 * KBLOCK].astype(BF16)
     tmp[...] = jnp.zeros_like(tmp)
     for h in range(3):
@@ -130,11 +194,10 @@
     rot_w[...] = tmp[0:80, 0:80].astype(BF16)
     tmp[...] = jnp.zeros_like(tmp)
     for f in range(4):
-        block = lift_ref[f]
-        tmp[0:BASIS, f * FROWS : f * FROWS + FACE] = block
-        tmp[0:BASIS, 96 + f * FROWS : 96 + f * FROWS + FACE] = low_of(block)
-        tmp[0:BASIS, 192 + f * FROWS : 192 + f * FROWS + FACE] = block
-    lift_w[...] = tmp[0:64, 0:288].astype(BF16)
+        for i in range(FACE):
+            tmp[f * FROWS + i : f * FROWS + i + 1, 0:BASIS] = lift_ref[i, f : f + 1, :]
+    high = tmp[0:96, 0:BASIS]
+    lift_w[...] = jnp.transpose(jnp.concatenate([high, low_of(high), high], axis=0)).astype(BF16)
 
     face_rows = lax.broadcasted_iota(jnp.int32, (FACES, ELEMS), 0)
     for f in range(4):
@@ -156,8 +219,9 @@
     take_w[...] = jnp.concatenate(take_parts, axis=0).astype(BF16)
 
     hot = lax.broadcasted_iota(jnp.int32, (16, ELEMS), 0) == mid_ref[...]
+    table = jnp.transpose(mat_ref[...])
     density, lame, shear = [
-        jnp.sum(jnp.where(hot, mat_ref[:, j : j + 1], 0.0), axis=0, keepdims=True) for j in range(3)
+        jnp.sum(jnp.where(hot, table[:, j : j + 1], 0.0), axis=0, keepdims=True) for j in range(3)
     ]
     inverse = 1.0 / density
     jac = [[jac_ref[d, k : k + 1, :] for k in range(3)] for d in range(3)]
@@ -227,7 +291,7 @@
         for d in range(8):
             send_buf[step, d] = outgoing[d * SLOTS : (d + 1) * SLOTS]
         if step == 0:
-            pl.semaphore_wait(barrier, 8)
+            pl.semaphore_wait(barrier, peers)
         copies = []
         for d in range(8):
             copy = pltpu.make_async_remote_copy(
@@ -238,8 +302,8 @@
                 device_id=partners[d],
                 device_id_type=MESH,
             )
-            copy.start()
             copies.append(copy)
+            pl.when(exists[d])(copy.start)
 
         slopes = dot(stiff_w[...], whole)
         volume = stress_from(slopes[:, 6 * ELEMS :], -1.0) + speed_from(slopes[:, : 6 * ELEMS], -1.0)
@@ -247,8 +311,8 @@
             out_ref[q] = current[q] + volume[q]
         beside = dot(faces_high, near_w[...]) + dot(faces_low, near_w[...])
 
-        for copy in copies:
-            copy.wait_recv()
+        for d in range(8):
+            pl.when(exists[7 - d])(copies[d].wait_recv)
         got = jnp.transpose(
             jnp.concatenate([recv_buf[step, d] for d in range(8)], axis=0)
         )
@@ -273,7 +337,7 @@
         fluxes = [[] for _ in range(QUANT)]
         for f in range(4):
             here = slice(f * ELEMS, (f + 1) * ELEMS)
-            n = [nrm_ref[f, k : k + 1, :] for k in range(3)]
+            n = [nrm_ref[k, f : f + 1, :] for k in range(3)]
             both = []
             apart = []
             for q in range(QUANT):
@@ -304,9 +368,9 @@
             lift_w[...], stacked([jnp.concatenate(parts, axis=0) for parts in fluxes], 96)
         )
         for q in range(QUANT):
-            out_ref[q] = out_ref[q] - lifted[0:BASIS, q * ELEMS : (q + 1) * ELEMS]
-        for copy in copies:
-            copy.wait_send()
+            out_ref[q] = out_ref[q] - lifted[:, q * ELEMS : (q + 1) * ELEMS]
+        for d in range(8):
+            pl.when(exists[d])(copies[d].wait_send)
 
 
 def solution(mesh):
@@ -314,19 +378,25 @@
 
     def per_device(*args):
         args = list(args)
+        args[3] = args[3].transpose(1, 0, 2)
+        args[4] = args[4].transpose(2, 0, 1)
+        args[6] = args[6].transpose(1, 0)
         args[7] = args[7].reshape(1, ELEMS)
+        args[9] = args[9].transpose(1, 0, 2)
         vmem = pl.BlockSpec(memory_space=pltpu.VMEM)
         return pl.pallas_call(
             functools.partial(kernel, rows, cols),
             out_shape=jax.ShapeDtypeStruct((QUANT, BASIS, ELEMS), F32),
-            in_specs=[vmem] * 15,
+            in_specs=[pl.BlockSpec(memory_space=pltpu.HBM)] * 15,
             out_specs=vmem,
-            scratch_shapes=[
+            scratch_shapes=[pltpu.VMEM(x.shape, x.dtype) for x in args]
+            + [
+                pltpu.SemaphoreType.DMA((15,)),
                 pltpu.VMEM((176, 384), F32),
                 pltpu.VMEM((176, 3 * KBLOCK), BF16),
                 pltpu.VMEM((176, 3 * KBLOCK), BF16),
                 pltpu.VMEM((96, 3 * KBLOCK), BF16),
-                pltpu.VMEM((64, 288), BF16),
+                pltpu.VMEM((BASIS, 288), BF16),
                 pltpu.VMEM((80, 80), BF16),
                 pltpu.VMEM((FACES, FACES), BF16),
                 pltpu.VMEM((8 * SLOTS, FACES), BF16),
@@ -337,7 +407,7 @@
                 pltpu.SemaphoreType.DMA((STEPS, 8)),
             ],
             compiler_params=pltpu.CompilerParams(
-                collective_id=0, has_side_effects=True, vmem_limit_bytes=40 * 1024 * 1024
+                collective_id=0, has_side_effects=True, vmem_limit_bytes=63 * 1024 * 1024
             ),
         )(*args)
 

time: 40.8 us -> 27.6 us (0.68)
  the two profiles are of different devices: /device:TPU:24 before, /device:TPU:1 now
where the time goes in v2:
time: 27.6 us; the launch traced here: 27.4 us
  Pallas kernels  25.8 us (93%)
  local copies, waits for them, and re-layouts  1.66 us (6%)
    pallas_call x1, Pallas kernels, per_device(): pl.pallas_call(functools.partial(kernel, rows, cols), out_shape=jax.Shape...  25.8 us
    unnamed x1, local copies, waits for them, and re-layouts  1.66 us

profile of v2, /device:TPU:1, one launch (start us, length us, event | category | flops | bytes accessed | tf_op | source)
XLA Modules:
  0.0 27.4 jit_solution(5845671374145722103)
XLA Ops:
  0.0 25.8 %shard_map.145 = f32[9,56,128]{2,1,0:T(8,128)} custom-call(f32[9,56,128]{2,1,0:T(8,128)} %dof_hbm.1, f32[3,56,56]{2,1,0:T(8,128)} %grad_hbm.1, f32[3,56,56]{2,1,0:T(8,128)} %stiff_hbm.1, f32[21,4,56]{2,1,0:T(4,128)} %bitcast.5, f32[21,4,56]{2,1,0:T(4,128)} %bitcast.6, f32[3,21,21]{2,1,0:T(8,128)} %rot_hbm.1, f32[3,16]{1,0:T(4,128)} %bitcast.8, ...), custom_call_target="tpu_custom_call" | custom-call | tf_op jit(solution)/shard_map/pallas_call | solution.py:387
  25.8 1.7 %copy.17 = f32[9,56,128]{2,1,0:T(8,128)} copy(f32[9,56,128]{2,1,0:T(8,128)} %shard_map.145) | data formatting | bytes 516096

commit v3 on v2

--- a/solution.py
+++ b/solution.py
@@ -11,6 +11,7 @@
 STEPS = 2
 TIME_STEP = 0.8
 OFFSETS = ((-1, -1), (-1, 0), (-1, 1), (0, -1), (0, 1), (1, -1), (1, 0), (1, 1))
+FAR_FIRST = (0, 2, 5, 7, 3, 4, 1, 6)
 MESH = pl.DeviceIdType.MESH
 F32 = jnp.float32
 BF16 = jnp.bfloat16
@@ -23,6 +24,25 @@
 FACES = 4 * ELEMS
 SLOTS = 24
 WIDE = 256
+
+
+(
+    GRAD,
+    DOF,
+    JAC,
+    MAT,
+    MID,
+    PROJ,
+    SEND_LIST,
+    STIFF,
+    LIFT,
+    ROT,
+    NRM,
+    ORI,
+    NEAR,
+    NEAR_FACE,
+    RECV_LIST,
+) = range(15)
 
 
 def dot(a, b):
@@ -166,109 +186,127 @@
             for step in range(STEPS):
                 recv_buf[step, d] = jnp.zeros((SLOTS, WIDE), F32)
 
+    def arrived(*names):
+        for name in names:
+            loads[name].wait()
+
+    def split_store(at, block, step_k):
+        height, width = block.shape
+        low = low_of(block)
+        tmp[at : at + height, 0:width] = block
+        tmp[at : at + height, step_k : step_k + width] = low
+        tmp[at : at + height, 2 * step_k : 2 * step_k + width] = block
+
+    def derivative_matrix(source, dest):
+        for block in range(7):
+            for d in range(3):
+                split_store(block * 24 + d * 8, source[d, block * 8 : block * 8 + 8], KBLOCK)
+        dest[...] = tmp[0:176, 0 : 3 * KBLOCK].astype(BF16)
+
+    def face_matrix(source):
+        for f in range(4):
+            for i in range(FACE):
+                tmp[f * FROWS + i : f * FROWS + i + 1, 0:BASIS] = source[i, f : f + 1, :]
+
+    def one_hot(ids_ref, dest, keep):
+        ids = jnp.transpose(ids_ref[0, 0])
+        face_ids = lax.broadcasted_iota(jnp.int32, (SLOTS, FACES), 1)
+        parts = []
+        for d in range(8):
+            hit = ids[:, d : d + 1] == face_ids
+            if keep is not None:
+                hit = hit & keep
+            parts.append(jnp.where(hit, 1.0, 0.0).astype(F32))
+        dest[...] = jnp.concatenate(parts, axis=0).astype(BF16)
+
     tmp[...] = jnp.zeros_like(tmp)
-    for load in loads:
-        load.wait()
-
-    def split_store(dest, at, block, step_k, first=True):
-        height, width = block.shape
-        dest[at : at + height, 0:width] = block
-        dest[at : at + height, step_k : step_k + width] = low_of(block)
-        dest[at : at + height, 2 * step_k : 2 * step_k + width] = block
-
-    for d in range(3):
-        split_store(tmp, d * BASIS, grad_ref[d], KBLOCK)
-    grad_w[...] = tmp[0:176, 0 : 3 * KBLOCK].astype(BF16)
-    for d in range(3):
-        split_store(tmp, d * BASIS, stiff_ref[d], KBLOCK)
-    stiff_w[...] = tmp[0:176, 0 : 3 * KBLOCK].astype(BF16)
-    tmp[...] = jnp.zeros_like(tmp)
-    for f in range(4):
-        for i in range(FACE):
-            tmp[f * FROWS + i : f * FROWS + i + 1, 0:BASIS] = proj_ref[i, f : f + 1, :]
-    split_store(tmp, 0, tmp[0:96, 0:KBLOCK], KBLOCK)
-    proj_w[...] = tmp[0:96, 0 : 3 * KBLOCK].astype(BF16)
-    tmp[...] = jnp.zeros_like(tmp)
-    for h in range(3):
-        split_store(tmp, h * FROWS, rot_ref[h], FROWS)
-    rot_w[...] = tmp[0:80, 0:80].astype(BF16)
-    tmp[...] = jnp.zeros_like(tmp)
-    for f in range(4):
-        for i in range(FACE):
-            tmp[f * FROWS + i : f * FROWS + i + 1, 0:BASIS] = lift_ref[i, f : f + 1, :]
-    high = tmp[0:96, 0:BASIS]
-    lift_w[...] = jnp.transpose(jnp.concatenate([high, low_of(high), high], axis=0)).astype(BF16)
-
-    face_rows = lax.broadcasted_iota(jnp.int32, (FACES, ELEMS), 0)
-    for f in range(4):
-        near = near_ref[f : f + 1, :]
-        source = jnp.where(near >= 0, near_face_ref[f : f + 1, :] * ELEMS + near, -1)
-        near_w[:, f * ELEMS : (f + 1) * ELEMS] = (face_rows == source).astype(F32).astype(BF16)
-    outside = jnp.concatenate([near_ref[f : f + 1, :] < 0 for f in range(4)], axis=1)
-    face_ids = lax.broadcasted_iota(jnp.int32, (SLOTS, FACES), 1)
-    give_ids = jnp.transpose(send_list_ref[0, 0])
-    take_ids = jnp.transpose(recv_list_ref[0, 0])
-    give_parts = []
-    take_parts = []
-    for d in range(8):
-        give_parts.append((give_ids[:, d : d + 1] == face_ids).astype(F32))
-        take_parts.append(
-            jnp.where((take_ids[:, d : d + 1] == face_ids) & outside, 1.0, 0.0).astype(F32)
-        )
-    give_w[...] = jnp.concatenate(give_parts, axis=0).astype(BF16)
-    take_w[...] = jnp.concatenate(take_parts, axis=0).astype(BF16)
-
+    arrived(GRAD)
+    derivative_matrix(grad_ref, grad_w)
+
+    arrived(JAC, MAT, MID)
     hot = lax.broadcasted_iota(jnp.int32, (16, ELEMS), 0) == mid_ref[...]
     table = jnp.transpose(mat_ref[...])
     density, lame, shear = [
         jnp.sum(jnp.where(hot, table[:, j : j + 1], 0.0), axis=0, keepdims=True) for j in range(3)
     ]
     inverse = 1.0 / density
-    jac = [[jac_ref[d, k : k + 1, :] for k in range(3)] for d in range(3)]
+    lame8, shear8, inverse8 = [
+        jnp.broadcast_to(x, (8, ELEMS)) for x in (lame, shear, inverse)
+    ]
+    jac = [
+        [jnp.broadcast_to(jac_ref[d, k : k + 1, :], (8, ELEMS)) for k in range(3)]
+        for d in range(3)
+    ]
+    arrived(DOF)
     root = jnp.sqrt((lame + 2.0 * shear) * inverse)
-    orient = jnp.concatenate([ori_ref[f : f + 1, :] for f in range(4)], axis=1)
-
-    def along(slopes, columns):
+
+    def along(slopes, block):
         def one(place, k):
             parts = [
                 jac[d][k]
-                * slopes[d * BASIS : (d + 1) * BASIS, place * ELEMS : (place + 1) * ELEMS]
+                * slopes[
+                    block * 24 + d * 8 : block * 24 + d * 8 + 8,
+                    place * ELEMS : (place + 1) * ELEMS,
+                ]
                 for d in range(3)
             ]
             return parts[0] + parts[1] + parts[2]
 
         return one
 
+    def by_blocks(rates):
+        return [jnp.concatenate(list(x), axis=0) for x in zip(*[rates(b) for b in range(7)])]
+
     def stress_from(slopes, scale):
-        one = along(slopes, 3)
-        ux, vy, wz = one(0, 0), one(1, 1), one(2, 2)
-        uv = one(1, 0) + one(0, 1)
-        vw = one(2, 1) + one(1, 2)
-        uw = one(2, 0) + one(0, 2)
-        return stress_rates(
-            ux, vy, wz, uv, vw, uw, scale * lame, (2.0 * scale) * shear, scale * shear
-        )
+        lame_s, shear2_s, shear_s = scale * lame8, (2.0 * scale) * shear8, scale * shear8
+
+        def rates(block):
+            one = along(slopes, block)
+            ux, vy, wz = one(0, 0), one(1, 1), one(2, 2)
+            uv = one(1, 0) + one(0, 1)
+            vw = one(2, 1) + one(1, 2)
+            uw = one(2, 0) + one(0, 2)
+            return stress_rates(ux, vy, wz, uv, vw, uw, lame_s, shear2_s, shear_s)
+
+        return by_blocks(rates)
 
     def speed_from(slopes, scale):
-        one = along(slopes, 6)
-        over = scale * inverse
-        return [
-            over * (one(0, 0) + one(3, 1) + one(5, 2)),
-            over * (one(3, 0) + one(1, 1) + one(4, 2)),
-            over * (one(5, 0) + one(4, 1) + one(2, 2)),
-        ]
+        over = scale * inverse8
+
+        def rates(block):
+            one = along(slopes, block)
+            return [
+                over * (one(0, 0) + one(3, 1) + one(5, 2)),
+                over * (one(3, 0) + one(1, 1) + one(4, 2)),
+                over * (one(5, 0) + one(4, 1) + one(2, 2)),
+            ]
+
+        return by_blocks(rates)
 
     for step in range(STEPS):
         current = dof_ref if step == 0 else out_ref
         level = [TIME_STEP * current[q] for q in range(QUANT)]
         total = list(level)
+        of_speed = dot(grad_w[...], stacked(level[6:], KBLOCK))
+        of_stress = dot(grad_w[...], stacked(level[:6], KBLOCK))
         for power in range(1, ORDER):
             scale = TIME_STEP / (power + 1)
-            from_stress = dot(grad_w[...], stacked(level[:6], KBLOCK))
-            from_speed = dot(grad_w[...], stacked(level[6:], KBLOCK))
-            level = stress_from(from_speed, scale) + speed_from(from_stress, scale)
-            total = [t + x for t, x in zip(total, level)]
-
+            stress = stress_from(of_speed, scale)
+            if power < ORDER - 1:
+                next_of_stress = dot(grad_w[...], stacked(stress, KBLOCK))
+            speed = speed_from(of_stress, scale)
+            if power < ORDER - 1:
+                of_speed = dot(grad_w[...], stacked(speed, KBLOCK))
+                of_stress = next_of_stress
+            total = [t + x for t, x in zip(total, stress + speed)]
+
+        if step == 0:
+            arrived(PROJ, SEND_LIST)
+            tmp[...] = jnp.zeros_like(tmp)
+            face_matrix(proj_ref)
+            split_store(0, tmp[0:96, 0:KBLOCK], KBLOCK)
+            proj_w[...] = tmp[0:96, 0 : 3 * KBLOCK].astype(BF16)
+            one_hot(send_list_ref, give_w, None)
         whole = stacked(total, KBLOCK)
         own = dot(proj_w[...], whole)
         faces = jnp.concatenate(
@@ -292,8 +330,8 @@
             send_buf[step, d] = outgoing[d * SLOTS : (d + 1) * SLOTS]
         if step == 0:
             pl.semaphore_wait(barrier, peers)
-        copies = []
-        for d in range(8):
+        copies = [None] * 8
+        for d in FAR_FIRST:
             copy = pltpu.make_async_remote_copy(
                 src_ref=send_buf.at[step, d],
                 dst_ref=recv_buf.at[step, 7 - d],
@@ -302,9 +340,32 @@
                 device_id=partners[d],
                 device_id_type=MESH,
             )
-            copies.append(copy)
+            copies[d] = copy
             pl.when(exists[d])(copy.start)
 
+        if step == 0:
+            arrived(STIFF, LIFT, ROT, NRM, ORI, NEAR, NEAR_FACE, RECV_LIST)
+            derivative_matrix(stiff_ref, stiff_w)
+            tmp[...] = jnp.zeros_like(tmp)
+            for h in range(3):
+                split_store(h * FROWS, rot_ref[h], FROWS)
+            rot_w[...] = tmp[0:80, 0:80].astype(BF16)
+            tmp[...] = jnp.zeros_like(tmp)
+            face_matrix(lift_ref)
+            high = tmp[0:96, 0:BASIS]
+            lift_w[...] = jnp.transpose(
+                jnp.concatenate([high, low_of(high), high], axis=0)
+            ).astype(BF16)
+            face_rows = lax.broadcasted_iota(jnp.int32, (FACES, ELEMS), 0)
+            for f in range(4):
+                near = near_ref[f : f + 1, :]
+                source = jnp.where(near >= 0, near_face_ref[f : f + 1, :] * ELEMS + near, -1)
+                near_w[:, f * ELEMS : (f + 1) * ELEMS] = (
+                    (face_rows == source).astype(F32).astype(BF16)
+                )
+            outside = jnp.concatenate([near_ref[f : f + 1, :] < 0 for f in range(4)], axis=1)
+            one_hot(recv_list_ref, take_w, outside)
+        orient = jnp.concatenate([ori_ref[f : f + 1, :] for f in range(4)], axis=1)
         slopes = dot(stiff_w[...], whole)
         volume = stress_from(slopes[:, 6 * ELEMS :], -1.0) + speed_from(slopes[:, : 6 * ELEMS], -1.0)
         for q in range(QUANT):
@@ -386,7 +447,7 @@
         vmem = pl.BlockSpec(memory_space=pltpu.VMEM)
         return pl.pallas_call(
             functools.partial(kernel, rows, cols),
-            out_shape=jax.ShapeDtypeStruct((QUANT, BASIS, ELEMS), F32),
+            out_shape=pltpu.VMEM((QUANT, BASIS, ELEMS), F32),
             in_specs=[pl.BlockSpec(memory_space=pltpu.HBM)] * 15,
             out_specs=vmem,
             scratch_shapes=[pltpu.VMEM(x.shape, x.dtype) for x in args]
@@ -407,9 +468,9 @@
                 pltpu.SemaphoreType.DMA((STEPS, 8)),
             ],
             compiler_params=pltpu.CompilerParams(
-                collective_id=0, has_side_effects=True, vmem_limit_bytes=63 * 1024 * 1024
+                collective_id=0, has_side_effects=True, vmem_limit_bytes=40 * 1024 * 1024
             ),
-        )(*args)
+        )(*[pltpu.with_memory_space_constraint(x, pltpu.HBM) for x in args])
 
     both = ("prow", "pcol")
     return jax.shard_map(

time: 27.6 us -> 25.2 us (0.913)
  Pallas kernels: 25.8 us -> 24.3 us
  local copies, waits for them, and re-layouts: 1.66 us -> 0.7 us
    pallas_call x1, Pallas kernels: 25.8 us -> 24.3 us  [per_device(): pl.pallas_call(functools.partial(kernel, rows, cols), out_shape=pltpu.VME...]
    unnamed x1, local copies, waits for them, and re-layouts: 1.66 us -> 0.7 us
where the time goes in v3:
time: 25.2 us; the launch traced here: 25 us
  Pallas kernels  24.3 us (96%)
  local copies, waits for them, and re-layouts  0.7 us (3%)
    pallas_call x1, Pallas kernels, per_device(): pl.pallas_call(functools.partial(kernel, rows, cols), out_shape=pltpu.VME...  24.3 us
    unnamed x1, local copies, waits for them, and re-layouts  0.7 us

profile of v3, /device:TPU:1, one launch (start us, length us, event | category | flops | bytes accessed | tf_op | source)
XLA Modules:
  0.0 25.0 jit_solution(8215002581835300321)
XLA Ops:
  0.0 24.3 %shard_map.145 = f32[9,56,128]{2,1,0:T(8,128)S(1)} custom-call(f32[9,56,128]{2,1,0:T(8,128)} %dof_hbm.1, f32[3,56,56]{2,1,0:T(8,128)} %grad_hbm.1, f32[3,56,56]{2,1,0:T(8,128)} %stiff_hbm.1, f32[21,4,56]{2,1,0:T(4,128)} %bitcast.5, f32[21,4,56]{2,1,0:T(4,128)} %bitcast.6, f32[3,21,21]{2,1,0:T(8,128)} %rot_hbm.1, f32[3,16]{1,0:T(4,128)} %bitcast.8, ...), custom_call_target="tpu_custom_call" | custom-call | tf_op jit(solution)/shard_map/pallas_call | solution.py:448
  24.3 0.7 %copy.17 = f32[9,56,128]{2,1,0:T(8,128)} copy(f32[9,56,128]{2,1,0:T(8,128)S(1)} %shard_map.145) | data formatting | bytes 516096

commit v4 on v3

--- a/solution.py
+++ b/solution.py
@@ -23,7 +23,10 @@
 ELEMS = 128
 FACES = 4 * ELEMS
 SLOTS = 24
-WIDE = 256
+FIRST = 128
+REST = 64
+HALF = 12
+HROWS = 16
 
 
 (
@@ -124,13 +127,19 @@
     grad_w,
     stiff_w,
     proj_w,
+    last_w,
     lift_w,
     rot_w,
+    rot_last_w,
     near_w,
     give_w,
+    give_half_w,
     take_w,
-    send_buf,
-    recv_buf,
+    take_half_w,
+    send_first,
+    send_rest,
+    recv_first,
+    recv_rest,
     send_sem,
     recv_sem,
 ):
@@ -184,7 +193,8 @@
         @pl.when(jnp.logical_not(exists[d]))
         def _(d=d):
             for step in range(STEPS):
-                recv_buf[step, d] = jnp.zeros((SLOTS, WIDE), F32)
+                recv_first[step, d] = jnp.zeros((SLOTS, ELEMS), F32)
+                recv_rest[step, d] = jnp.zeros((HROWS, ELEMS), F32)
 
     def arrived(*names):
         for name in names:
@@ -208,16 +218,20 @@
             for i in range(FACE):
                 tmp[f * FROWS + i : f * FROWS + i + 1, 0:BASIS] = source[i, f : f + 1, :]
 
-    def one_hot(ids_ref, dest, keep):
-        ids = jnp.transpose(ids_ref[0, 0])
-        face_ids = lax.broadcasted_iota(jnp.int32, (SLOTS, FACES), 1)
+    def one_hot(columns, dest, keep):
         parts = []
-        for d in range(8):
-            hit = ids[:, d : d + 1] == face_ids
-            if keep is not None:
-                hit = hit & keep
-            parts.append(jnp.where(hit, 1.0, 0.0).astype(F32))
+        for part in columns:
+            face_ids = lax.broadcasted_iota(jnp.int32, (part.shape[0], FACES), 1)
+            for d in range(8):
+                hit = part[:, d : d + 1] == face_ids
+                if keep is not None:
+                    hit = hit & keep
+                parts.append(jnp.where(hit, 1.0, 0.0).astype(F32))
         dest[...] = jnp.concatenate(parts, axis=0).astype(BF16)
+
+    def halves(ids):
+        none = jnp.full((HROWS - HALF, 8), -1, jnp.int32)
+        return [jnp.concatenate([ids[at : at + HALF], none], axis=0) for at in (0, HALF)]
 
     tmp[...] = jnp.zeros_like(tmp)
     arrived(GRAD)
@@ -237,7 +251,7 @@
         [jnp.broadcast_to(jac_ref[d, k : k + 1, :], (8, ELEMS)) for k in range(3)]
         for d in range(3)
     ]
-    arrived(DOF)
+    arrived(DOF, PROJ, SEND_LIST)
     root = jnp.sqrt((lame + 2.0 * shear) * inverse)
 
     def along(slopes, block):
@@ -301,47 +315,65 @@
             total = [t + x for t, x in zip(total, stress + speed)]
 
         if step == 0:
-            arrived(PROJ, SEND_LIST)
             tmp[...] = jnp.zeros_like(tmp)
             face_matrix(proj_ref)
             split_store(0, tmp[0:96, 0:KBLOCK], KBLOCK)
             proj_w[...] = tmp[0:96, 0 : 3 * KBLOCK].astype(BF16)
-            one_hot(send_list_ref, give_w, None)
+            tmp[...] = jnp.zeros_like(tmp)
+            for f in range(4):
+                for i in range(FACE):
+                    at = (f * 7 + i // 3) * 8 + 5 + i % 3
+                    tmp[at : at + 1, 0:BASIS] = proj_ref[i, f : f + 1, :]
+            split_store(0, tmp[0:224, 0:KBLOCK], KBLOCK)
+            last_w[...] = tmp[0:224, 0 : 3 * KBLOCK].astype(BF16)
+            give_ids = jnp.transpose(send_list_ref[0, 0])
+            one_hot([give_ids], give_w, None)
         whole = stacked(total, KBLOCK)
         own = dot(proj_w[...], whole)
-        faces = jnp.concatenate(
-            [
-                jnp.concatenate(
-                    [
-                        own[f * FROWS : (f + 1) * FROWS, q * ELEMS : (q + 1) * ELEMS]
-                        for f in range(4)
-                    ],
-                    axis=1,
-                )
-                for q in range(QUANT)
-            ]
-            + [jnp.zeros((WIDE - QUANT * FROWS, FACES), F32)],
-            axis=0,
-        )
+        spare = dot(last_w[...], whole[:, (QUANT - 1) * ELEMS :])
+        faces = []
+        for q in range(QUANT - 1):
+            row_of = []
+            for f in range(4):
+                block = own[f * FROWS : (f + 1) * FROWS, q * ELEMS : (q + 1) * ELEMS]
+                if q < 7:
+                    at = (f * 7 + q) * 8
+                    block = jnp.concatenate([block[0:16], block[16:24] + spare[at : at + 8]], axis=0)
+                row_of.append(block)
+            faces.append(jnp.concatenate(row_of, axis=1))
+        faces = jnp.concatenate(faces, axis=0)
         faces_high = faces.astype(BF16)
         faces_low = (faces - faces_high.astype(F32)).astype(BF16)
-        outgoing = dot_nt(give_w[...], faces_high) + dot_nt(give_w[...], faces_low)
+        outgoing = dot_nt(give_w[...], faces_high[0:FIRST]) + dot_nt(give_w[...], faces_low[0:FIRST])
         for d in range(8):
-            send_buf[step, d] = outgoing[d * SLOTS : (d + 1) * SLOTS]
+            send_first[step, d] = outgoing[d * SLOTS : (d + 1) * SLOTS]
         if step == 0:
             pl.semaphore_wait(barrier, peers)
-        copies = [None] * 8
-        for d in FAR_FIRST:
-            copy = pltpu.make_async_remote_copy(
-                src_ref=send_buf.at[step, d],
-                dst_ref=recv_buf.at[step, 7 - d],
-                send_sem=send_sem.at[step, d],
-                recv_sem=recv_sem.at[step, 7 - d],
-                device_id=partners[d],
-                device_id_type=MESH,
-            )
-            copies[d] = copy
-            pl.when(exists[d])(copy.start)
+        copies = {}
+
+        def send(source, dest, part):
+            for d in FAR_FIRST:
+                copy = pltpu.make_async_remote_copy(
+                    src_ref=source.at[step, d],
+                    dst_ref=dest.at[step, 7 - d],
+                    send_sem=send_sem.at[step, part, d],
+                    recv_sem=recv_sem.at[step, part, 7 - d],
+                    device_id=partners[d],
+                    device_id_type=MESH,
+                )
+                copies[part, d] = copy
+                pl.when(exists[d])(copy.start)
+
+        send(send_first, recv_first, 0)
+        if step == 0:
+            one_hot(halves(give_ids), give_half_w, None)
+        outgoing = dot_nt(give_half_w[...], faces_high[FIRST:]) + dot_nt(
+            give_half_w[...], faces_low[FIRST:]
+        )
+        outgoing = jnp.concatenate([outgoing[0:128], outgoing[128:256]], axis=1)
+        for d in range(8):
+            send_rest[step, d] = outgoing[d * HROWS : (d + 1) * HROWS]
+        send(send_rest, recv_rest, 1)
 
         if step == 0:
             arrived(STIFF, LIFT, ROT, NRM, ORI, NEAR, NEAR_FACE, RECV_LIST)
@@ -350,6 +382,16 @@
             for h in range(3):
                 split_store(h * FROWS, rot_ref[h], FROWS)
             rot_w[...] = tmp[0:80, 0:80].astype(BF16)
+            tmp[...] = jnp.zeros_like(tmp)
+            for h in range(3):
+                back = jnp.transpose(rot_ref[h])
+                for i in range(FACE):
+                    at = (i // 3) * 8 + 5 + i % 3
+                    tmp[at : at + 1, h * FROWS : h * FROWS + FACE] = back[i : i + 1, :]
+            last = jnp.transpose(tmp[0:BASIS, 0:ELEMS])[0:80]
+            tmp[...] = jnp.zeros_like(tmp)
+            split_store(0, last, BASIS)
+            rot_last_w[...] = tmp[0:80, 0:176].astype(BF16)
             tmp[...] = jnp.zeros_like(tmp)
             face_matrix(lift_ref)
             high = tmp[0:96, 0:BASIS]
@@ -364,7 +406,9 @@
                     (face_rows == source).astype(F32).astype(BF16)
                 )
             outside = jnp.concatenate([near_ref[f : f + 1, :] < 0 for f in range(4)], axis=1)
-            one_hot(recv_list_ref, take_w, outside)
+            take_ids = jnp.transpose(recv_list_ref[0, 0])
+            one_hot([take_ids], take_w, outside)
+            one_hot(halves(take_ids), take_half_w, outside)
         orient = jnp.concatenate([ori_ref[f : f + 1, :] for f in range(4)], axis=1)
         slopes = dot(stiff_w[...], whole)
         volume = stress_from(slopes[:, 6 * ELEMS :], -1.0) + speed_from(slopes[:, : 6 * ELEMS], -1.0)
@@ -372,21 +416,33 @@
             out_ref[q] = current[q] + volume[q]
         beside = dot(faces_high, near_w[...]) + dot(faces_low, near_w[...])
 
-        for d in range(8):
-            pl.when(exists[7 - d])(copies[d].wait_recv)
-        got = jnp.transpose(
-            jnp.concatenate([recv_buf[step, d] for d in range(8)], axis=0)
-        )
-        got_high = got.astype(BF16)
-        got_low = (got - got_high.astype(F32)).astype(BF16)
-        beside = beside + dot(got_high, take_w[...]) + dot(got_low, take_w[...])
+        for part in range(2):
+            for d in FAR_FIRST[::-1]:
+                pl.when(exists[7 - d])(copies[part, d].wait_recv)
+        first = jnp.transpose(jnp.concatenate([recv_first[step, d] for d in range(8)], axis=0))
+        rest = jnp.transpose(jnp.concatenate([recv_rest[step, d] for d in range(8)], axis=0))
+        rest = jnp.concatenate([rest[0:REST], rest[REST:]], axis=1)
+        arrived_faces = []
+        for got, take in ((first, take_w), (rest, take_half_w)):
+            got_high = got.astype(BF16)
+            got_low = (got - got_high.astype(F32)).astype(BF16)
+            arrived_faces.append(dot(got_high, take[...]) + dot(got_low, take[...]))
+        beside = beside + jnp.concatenate(arrived_faces, axis=0)
 
         turned = []
         for q in range(QUANT):
-            block = beside[q * FROWS : (q + 1) * FROWS]
-            low = low_of(block)
-            right = jnp.concatenate([block, block, low, jnp.zeros((8, FACES), F32)], axis=0)
-            each = dot(rot_w[...], right.astype(BF16))
+            if q < QUANT - 1:
+                block = beside[q * FROWS : (q + 1) * FROWS]
+                matrix = rot_w
+            else:
+                block = jnp.concatenate(
+                    [beside[b * FROWS + 16 : (b + 1) * FROWS] for b in range(7)], axis=0
+                )
+                matrix = rot_last_w
+            right = jnp.concatenate(
+                [block, block, low_of(block), jnp.zeros((8, FACES), F32)], axis=0
+            )
+            each = dot(matrix[...], right.astype(BF16))
             turned.append(
                 jnp.where(
                     orient == 0,
@@ -430,8 +486,9 @@
         )
         for q in range(QUANT):
             out_ref[q] = out_ref[q] - lifted[:, q * ELEMS : (q + 1) * ELEMS]
-        for d in range(8):
-            pl.when(exists[d])(copies[d].wait_send)
+        for part in range(2):
+            for d in range(8):
+                pl.when(exists[d])(copies[part, d].wait_send)
 
 
 def solution(mesh):
@@ -453,19 +510,25 @@
             scratch_shapes=[pltpu.VMEM(x.shape, x.dtype) for x in args]
             + [
                 pltpu.SemaphoreType.DMA((15,)),
-                pltpu.VMEM((176, 384), F32),
+                pltpu.VMEM((224, 384), F32),
                 pltpu.VMEM((176, 3 * KBLOCK), BF16),
                 pltpu.VMEM((176, 3 * KBLOCK), BF16),
                 pltpu.VMEM((96, 3 * KBLOCK), BF16),
+                pltpu.VMEM((224, 3 * KBLOCK), BF16),
                 pltpu.VMEM((BASIS, 288), BF16),
                 pltpu.VMEM((80, 80), BF16),
+                pltpu.VMEM((80, 176), BF16),
                 pltpu.VMEM((FACES, FACES), BF16),
                 pltpu.VMEM((8 * SLOTS, FACES), BF16),
+                pltpu.VMEM((2 * 8 * HROWS, FACES), BF16),
                 pltpu.VMEM((8 * SLOTS, FACES), BF16),
-                pltpu.VMEM((STEPS, 8, SLOTS, WIDE), F32),
-                pltpu.VMEM((STEPS, 8, SLOTS, WIDE), F32),
-                pltpu.SemaphoreType.DMA((STEPS, 8)),
-                pltpu.SemaphoreType.DMA((STEPS, 8)),
+                pltpu.VMEM((2 * 8 * HROWS, FACES), BF16),
+                pltpu.VMEM((STEPS, 8, SLOTS, ELEMS), F32),
+                pltpu.VMEM((STEPS, 8, HROWS, ELEMS), F32),
+                pltpu.VMEM((STEPS, 8, SLOTS, ELEMS), F32),
+                pltpu.VMEM((STEPS, 8, HROWS, ELEMS), F32),
+                pltpu.SemaphoreType.DMA((STEPS, 2, 8)),
+                pltpu.SemaphoreType.DMA((STEPS, 2, 8)),
             ],
             compiler_params=pltpu.CompilerParams(
                 collective_id=0, has_side_effects=True, vmem_limit_bytes=40 * 1024 * 1024

time: 25.2 us -> 25.7 us (1.020)
  Pallas kernels: 24.3 us -> 24.8 us
    pallas_call x1, Pallas kernels: 24.3 us -> 24.8 us  [per_device(): pl.pallas_call(functools.partial(kernel, rows, cols), out_shape=pltpu.VME...]
where the time goes in v4:
time: 25.7 us; the launch traced here: 25.5 us
  Pallas kernels  24.8 us (96%)
  local copies, waits for them, and re-layouts  0.7 us (3%)
    pallas_call x1, Pallas kernels, per_device(): pl.pallas_call(functools.partial(kernel, rows, cols), out_shape=pltpu.VME...  24.8 us
    unnamed x1, local copies, waits for them, and re-layouts  0.7 us

profile of v4, /device:TPU:1, one launch (start us, length us, event | category | flops | bytes accessed | tf_op | source)
XLA Modules:
  0.0 25.5 jit_solution(16186646276559925229)
XLA Ops:
  0.0 24.8 %shard_map.145 = f32[9,56,128]{2,1,0:T(8,128)S(1)} custom-call(f32[9,56,128]{2,1,0:T(8,128)} %dof_hbm.1, f32[3,56,56]{2,1,0:T(8,128)} %grad_hbm.1, f32[3,56,56]{2,1,0:T(8,128)} %stiff_hbm.1, f32[21,4,56]{2,1,0:T(4,128)} %bitcast.5, f32[21,4,56]{2,1,0:T(4,128)} %bitcast.6, f32[3,21,21]{2,1,0:T(8,128)} %rot_hbm.1, f32[3,16]{1,0:T(4,128)} %bitcast.8, ...), custom_call_target="tpu_custom_call" | custom-call | tf_op jit(solution)/shard_map/pallas_call | solution.py:505
  24.8 0.7 %copy.17 = f32[9,56,128]{2,1,0:T(8,128)} copy(f32[9,56,128]{2,1,0:T(8,128)S(1)} %shard_map.145) | data formatting | bytes 516096

commit v5 on v3

--- a/solution.py
+++ b/solution.py
@@ -237,7 +237,7 @@
         [jnp.broadcast_to(jac_ref[d, k : k + 1, :], (8, ELEMS)) for k in range(3)]
         for d in range(3)
     ]
-    arrived(DOF)
+    arrived(DOF, PROJ, SEND_LIST)
     root = jnp.sqrt((lame + 2.0 * shear) * inverse)
 
     def along(slopes, block):
@@ -301,7 +301,6 @@
             total = [t + x for t, x in zip(total, stress + speed)]
 
         if step == 0:
-            arrived(PROJ, SEND_LIST)
             tmp[...] = jnp.zeros_like(tmp)
             face_matrix(proj_ref)
             split_store(0, tmp[0:96, 0:KBLOCK], KBLOCK)
@@ -373,6 +372,8 @@
         beside = dot(faces_high, near_w[...]) + dot(faces_low, near_w[...])
 
         for d in range(8):
+            pl.when(exists[d])(copies[d].wait_send)
+        for d in FAR_FIRST[::-1]:
             pl.when(exists[7 - d])(copies[d].wait_recv)
         got = jnp.transpose(
             jnp.concatenate([recv_buf[step, d] for d in range(8)], axis=0)
@@ -430,8 +431,6 @@
         )
         for q in range(QUANT):
             out_ref[q] = out_ref[q] - lifted[:, q * ELEMS : (q + 1) * ELEMS]
-        for d in range(8):
-            pl.when(exists[d])(copies[d].wait_send)
 
 
 def solution(mesh):

time: 25.2 us -> 25 us (level)
  no operation moved by 1% of the time
where the time goes in v5:
time: 25 us; the launch traced here: 24.9 us
  Pallas kernels  24.2 us (97%)
  local copies, waits for them, and re-layouts  0.7 us (3%)
    pallas_call x1, Pallas kernels, per_device(): pl.pallas_call(functools.partial(kernel, rows, cols), out_shape=pltpu.VME...  24.2 us
    unnamed x1, local copies, waits for them, and re-layouts  0.7 us

profile of v5, /device:TPU:1, one launch (start us, length us, event | category | flops | bytes accessed | tf_op | source)
XLA Modules:
  0.0 24.9 jit_solution(2684895643191563872)
XLA Ops:
  0.0 24.2 %shard_map.145 = f32[9,56,128]{2,1,0:T(8,128)S(1)} custom-call(f32[9,56,128]{2,1,0:T(8,128)} %dof_hbm.1, f32[3,56,56]{2,1,0:T(8,128)} %grad_hbm.1, f32[3,56,56]{2,1,0:T(8,128)} %stiff_hbm.1, f32[21,4,56]{2,1,0:T(4,128)} %bitcast.5, f32[21,4,56]{2,1,0:T(4,128)} %bitcast.6, f32[3,21,21]{2,1,0:T(8,128)} %rot_hbm.1, f32[3,16]{1,0:T(4,128)} %bitcast.8, ...), custom_call_target="tpu_custom_call" | custom-call | tf_op jit(solution)/shard_map/pallas_call | solution.py:447
  24.2 0.7 %copy.17 = f32[9,56,128]{2,1,0:T(8,128)} copy(f32[9,56,128]{2,1,0:T(8,128)S(1)} %shard_map.145) | data formatting | bytes 516096

commit v6 on v5

--- a/solution.py
+++ b/solution.py
@@ -155,8 +155,9 @@
         ]
     ):
         load = pltpu.make_async_copy(source, dest, load_sem.at[at])
+        loads.append(load)
+    for load in loads[:2]:
         load.start()
-        loads.append(load)
 
     row = lax.axis_index("prow")
     col = lax.axis_index("pcol")
@@ -185,6 +186,9 @@
         def _(d=d):
             for step in range(STEPS):
                 recv_buf[step, d] = jnp.zeros((SLOTS, WIDE), F32)
+
+    for load in loads[2:]:
+        load.start()
 
     def arrived(*names):
         for name in names:

time: 25 us -> 25 us (level)
  no operation moved by 1% of the time
where the time goes in v6:
time: 25 us; the launch traced here: 24.9 us
  Pallas kernels  24.2 us (97%)
  local copies, waits for them, and re-layouts  0.7 us (3%)
    pallas_call x1, Pallas kernels, per_device(): pl.pallas_call(functools.partial(kernel, rows, cols), out_shape=pltpu.VME...  24.2 us
    unnamed x1, local copies, waits for them, and re-layouts  0.7 us

profile of v6, /device:TPU:1, one launch (start us, length us, event | category | flops | bytes accessed | tf_op | source)
XLA Modules:
  0.0 24.9 jit_solution(2783509698453913883)
XLA Ops:
  0.0 24.2 %shard_map.145 = f32[9,56,128]{2,1,0:T(8,128)S(1)} custom-call(f32[9,56,128]{2,1,0:T(8,128)} %dof_hbm.1, f32[3,56,56]{2,1,0:T(8,128)} %grad_hbm.1, f32[3,56,56]{2,1,0:T(8,128)} %stiff_hbm.1, f32[21,4,56]{2,1,0:T(4,128)} %bitcast.5, f32[21,4,56]{2,1,0:T(4,128)} %bitcast.6, f32[3,21,21]{2,1,0:T(8,128)} %rot_hbm.1, f32[3,16]{1,0:T(4,128)} %bitcast.8, ...), custom_call_target="tpu_custom_call" | custom-call | tf_op jit(solution)/shard_map/pallas_call | solution.py:451
  24.2 0.7 %copy.17 = f32[9,56,128]{2,1,0:T(8,128)} copy(f32[9,56,128]{2,1,0:T(8,128)S(1)} %shard_map.145) | data formatting | bytes 516096
